TPU v7x, 32 devices: a whole 2x2x4 slice. The times are simulated.
32 devices in a mesh: ctx: 4 (over y, core), grp: 8 (over z, x).
Axes of the slice: x: 2, y: 2, z: 4, core: 2. Of those that a mesh axis runs over, the one named last changes fastest.
Arguments:
- query_feat: bfloat16 [8192, 4096], P(('ctx', 'grp')), may hold values from 0.0099487305 to 1
- key_feat: bfloat16 [8192, 4096], P(('ctx', 'grp')), may hold values from 0.0099487305 to 1
- values: bfloat16 [8192, 2048], P(('ctx', 'grp')), may hold values from -6 to 6
- teacher: bfloat16 [8192, 2048], P('ctx', 'grp'), may hold values from -4 to 4
Outputs:
- query_grad: bfloat16 [8192, 4096], P(('ctx', 'grp'))
- key_grad: bfloat16 [8192, 4096], P(('ctx', 'grp'))
All inputs are finite; a program needn't handle non-finite values.
Results may differ from a plain program's by a relative error of at most 0.001.
Values may be sent and summed in bfloat16 or wider, within the bound.
A program may use at most 576 MiB of HBM per device.

v0:
```python
import jax
import jax.numpy as jnp
from jax import lax
from jax.sharding import PartitionSpec as P

H = 16


HIGH = lax.Precision.HIGHEST


def entering(array, axis, combine, identity, reverse):
    size, mine = (lax.axis_size(axis), lax.axis_index(axis))
    everything = jax.tree.map(lambda part: lax.all_gather(part, axis), array)
    start = jax.tree.map(
        lambda part, zero: jnp.broadcast_to(jnp.asarray(zero, part.dtype), part.shape),
        array,
        identity,
    )

    def step(k, before):
        at = size - 1 - k if reverse else k
        reached = at > mine if reverse else at < mine
        new = combine(before, jax.tree.map(lambda part: part[at], everything))
        return jax.tree.map(lambda a, b: jnp.where(reached, a, b), new, before)

    return lax.fori_loop(0, size, step, start)


def add_pair(earlier, later):
    return (earlier[0] + later[0], earlier[1] + later[1])


def exclusive_blocks(stack, reverse):
    return lax.cumsum(stack, axis=0, reverse=reverse) - stack


def local_grads(query_feat, key_feat, values, teacher, heads, before_fn, after_fn, scale):
    rows = query_feat.shape[0]
    feat = query_feat.shape[1] // heads
    width = values.shape[1] // heads
    block = min(rows, 512)
    count = rows // block
    fq = query_feat.reshape(count, block, heads, feat)
    fk = key_feat.reshape(count, block, heads, feat)
    fq_wide = fq.astype(jnp.float32)
    fk_wide = fk.astype(jnp.float32)
    val_wide = values.reshape(count, block, heads, width).astype(jnp.float32)
    target = teacher.reshape(count, block, heads, width).astype(jnp.float32)
    rows_t = lax.broadcasted_iota(jnp.int32, (block, block), 0)
    rows_s = lax.broadcasted_iota(jnp.int32, (block, block), 1)
    causal = (rows_s <= rows_t).astype(jnp.float32)
    scores = jnp.einsum("bthf,bshf->bhts", fq, fk, preferred_element_type=jnp.float32) * causal
    kv_blocks = jnp.einsum("bshf,bshd->bhfd", fk_wide, val_wide, precision=HIGH)
    key_blocks = jnp.sum(fk_wide, axis=1)
    kv_before, key_before = before_fn(jnp.sum(kv_blocks, axis=0), jnp.sum(key_blocks, axis=0))
    kv_state = kv_before[None] + exclusive_blocks(kv_blocks, False)
    key_state = key_before[None] + exclusive_blocks(key_blocks, False)
    numer = jnp.einsum("bhts,bshd->bthd", scores, val_wide, precision=HIGH)
    numer = numer + jnp.einsum("bthf,bhfd->bthd", fq_wide, kv_state, precision=HIGH)
    denom = jnp.transpose(jnp.sum(scores, axis=3), (0, 2, 1))
    denom = denom + jnp.einsum("bthf,bhf->bth", fq_wide, key_state, precision=HIGH)
    student = numer / denom[..., None]
    resid = student - target
    d_numer = resid / denom[..., None]
    d_denom = -jnp.sum(resid * student, axis=3) / denom
    mixed = jnp.einsum("bthd,bshd->bhts", d_numer, val_wide, precision=HIGH)
    mixed = (mixed + jnp.transpose(d_denom, (0, 2, 1))[..., None]) * causal
    adj_blocks = jnp.einsum("bthf,bthd->bhfd", fq_wide, d_numer, precision=HIGH)
    query_blocks = jnp.einsum("bthf,bth->bhf", fq_wide, d_denom, precision=HIGH)
    adj_after, query_after = after_fn(jnp.sum(adj_blocks, axis=0), jnp.sum(query_blocks, axis=0))
    adj_state = adj_after[None] + exclusive_blocks(adj_blocks, True)
    query_state = query_after[None] + exclusive_blocks(query_blocks, True)
    q_grad = jnp.einsum("bhts,bshf->bthf", mixed, fk_wide, precision=HIGH)
    q_grad = q_grad + jnp.einsum("bhfd,bthd->bthf", kv_state, d_numer, precision=HIGH)
    q_grad = q_grad + key_state[:, None] * d_denom[..., None]
    k_grad = jnp.einsum("bhts,bthf->bshf", mixed, fq_wide, precision=HIGH)
    k_grad = k_grad + jnp.einsum("bhfd,bshd->bshf", adj_state, val_wide, precision=HIGH)
    k_grad = k_grad + query_state[:, None]
    query_out = (scale * q_grad).astype(jnp.bfloat16).reshape(rows, heads * feat)
    key_out = (scale * k_grad).astype(jnp.bfloat16).reshape(rows, heads * feat)
    return (query_out, key_out)


def on_device(query_feat, key_feat, values, teacher):
    groups = lax.axis_size("grp")
    total_tokens = query_feat.shape[0] * lax.axis_size("ctx") * groups
    scale = float(total_tokens) ** 0.5
    query_rows, key_rows, value_rows = (
        lax.all_to_all(query_feat, "grp", split_axis=1, concat_axis=0, tiled=True),
        lax.all_to_all(key_feat, "grp", split_axis=1, concat_axis=0, tiled=True),
        lax.all_to_all(values, "grp", split_axis=1, concat_axis=0, tiled=True),
    )
    heads_here = H // groups

    def before_fn(kv_sum, key_sum):
        zeros = (jnp.zeros_like(kv_sum), jnp.zeros_like(key_sum))
        return entering((kv_sum, key_sum), "ctx", add_pair, zeros, False)

    def after_fn(adj_sum, query_sum):
        zeros = (jnp.zeros_like(adj_sum), jnp.zeros_like(query_sum))
        return entering((adj_sum, query_sum), "ctx", add_pair, zeros, True)

    query_head, key_head = local_grads(
        query_rows, key_rows, value_rows, teacher, heads_here, before_fn, after_fn, scale
    )
    query_grad, key_grad = (
        lax.all_to_all(query_head, "grp", split_axis=0, concat_axis=1, tiled=True),
        lax.all_to_all(key_head, "grp", split_axis=0, concat_axis=1, tiled=True),
    )
    return (query_grad, key_grad)


def solution(mesh):
    placed = (
        P(("ctx", "grp"), None),
        P(("ctx", "grp"), None),
        P(("ctx", "grp"), None),
        P("ctx", "grp"),
    )
    return jax.shard_map(
        on_device,
        mesh=mesh,
        in_specs=placed,
        out_specs=(P(("ctx", "grp"), None), P(("ctx", "grp"), None)),
        check_vma=False,
    )
```

profile of v0, /device:TPU:0, one launch (start us, length us, event | category | flops | bytes accessed | tf_op | source)
XLA Modules:
  0.0 338.0 jit_solution(8241884110436552563)
XLA Ops:
  9.6 7.3 %all-to-all-start.2 = ((bf16[256,8,256]{2,0,1:T(8,128)(2,1)}), bf16[256,8,256]{2,0,1:T(8,128)(2,1)S(1)}, u32[]{:S(2)}, u32[]{:S(2)}) async-start(bf16[256,8,256]{2,0,1:T(8,128)(2,1)} %bitcast.79), calls=%async_computation.2 | async-start | bytes 2097152 | tf_op jit(solution)/shard_map/all_to_all | solution.py:92
  18.4 24.2 %all-to-all-done.2 = bf16[256,8,256]{2,0,1:T(8,128)(2,1)S(1)} async-done(((bf16[256,8,256]{2,0,1:T(8,128)(2,1)}), bf16[256,8,256]{2,0,1:T(8,128)(2,1)S(1)}, u32[]{:S(2)}, u32[]{:S(2)}) %all-to-all-start.2) | async-done | bytes 1048608 | tf_op jit(solution)/shard_map/all_to_all | solution.py:92
  43.6 3.6 %all-to-all-start.1 = ((bf16[256,8,512]{2,0,1:T(8,128)(2,1)}), bf16[256,8,512]{2,0,1:T(8,128)(2,1)S(1)}, u32[]{:S(2)}, u32[]{:S(2)}) async-start(bf16[256,8,512]{2,0,1:T(8,128)(2,1)} %bitcast.94), calls=%async_computation.1 | async-start | bytes 4194304 | tf_op jit(solution)/shard_map/all_to_all | solution.py:91
  47.2 3.1 copy.245
  50.3 45.3 %all-to-all-done.1 = bf16[256,8,512]{2,0,1:T(8,128)(2,1)S(1)} async-done(((bf16[256,8,512]{2,0,1:T(8,128)(2,1)}), bf16[256,8,512]{2,0,1:T(8,128)(2,1)S(1)}, u32[]{:S(2)}, u32[]{:S(2)}) %all-to-all-start.1) | async-done | bytes 2097184 | tf_op jit(solution)/shard_map/all_to_all | solution.py:91
  96.9 4.3 %all-to-all-start = ((bf16[256,8,512]{2,0,1:T(8,128)(2,1)}), bf16[256,8,512]{2,0,1:T(8,128)(2,1)}, u32[]{:S(2)}, u32[]{:S(2)}) async-start(bf16[256,8,512]{2,0,1:T(8,128)(2,1)} %bitcast.92), calls=%async_computation | async-start | bytes 4194304 | tf_op jit(solution)/shard_map/all_to_all | solution.py:90
  102.7 2.9 reshape.64
  105.6 2.5 fusion.45
  112.8 36.3 %all-to-all-done = bf16[256,8,512]{2,0,1:T(8,128)(2,1)} async-done(((bf16[256,8,512]{2,0,1:T(8,128)(2,1)}), bf16[256,8,512]{2,0,1:T(8,128)(2,1)}, u32[]{:S(2)}, u32[]{:S(2)}) %all-to-all-start) | async-done | bytes 2097184 | tf_op jit(solution)/shard_map/all_to_all | solution.py:90
  149.1 2.5 reshape.63
  154.1 5.3 %all_gather.27 = f32[4,2,256]{2,1,0:T(2,128)S(1)} all-gather(f32[1,2,256]{2,1,0:T(2,128)S(1)} %all_gather.26), channel_id=1, replica_groups=mesh['ctx'=4,'grp'=8] {'ctx'}, dimensions={0}, use_global_device_ids=true | all-gather | bytes 10240 | tf_op jit(solution)/shard_map/all_gather | solution.py:14
  159.5 6.1 %multiply_reduce_fusion = (f32[4,2,512]{2,1,0:T(2,128)S(1)}, f32[4,2,512,512]{2,3,1,0:T(8,128)}) fusion(f32[512,512]{0,1:T(8,128)S(1)} %fusion.25, bf16[4,512,2,256]{3,2,1,0:T(2,128)(2,1)} %copy-done, bf16[4,512,2,256]{3,2,1,0:T(2,128)(2,1)S(1)} %reshape.63), kind=kOutput, calls=%fused_computation.5 | convolution fusion | flops 1077932032 | bytes 13647872 | tf_op jit(solution)/shard_map/bthf,bshf->bhts/dot_general | solution.py:53
  165.6 7.1 %while.34 = (s32[]{:T(128)}, f32[2,256,128]{2,1,0:T(8,128)}, f32[2,256]{1,0:T(2,128)S(1)}, s32[]{:T(128)}, f32[4,2,256,128]{3,2,1,0:T(8,128)}, /*index=5*/f32[4,2,256]{2,1,0:T(2,128)S(1)}, s32[]{:T(128)}, s32[]{:T(128)}) while((s32[]{:T(128)}, f32[2,256,128]{2,1,0:T(8,128)}, f32[2,256]{1,0:T(2,128)S(1)}, s32[]{:T(128)}, ...), condition=%wide.region_3.4_spmd.clone, body=%wide.region_2.0_spmd.clone.sunk | while | flops 198148 | bytes 792699 | solution.py:27
  178.2 7.4 %multiply_reduce_fusion.1 = (f32[4,512,2]{1,2,0:T(2,128)S(1)}, f32[4,512,2,128]{1,3,2,0:T(8,128)S(1)}) fusion(f32[4,512,2,128]{1,3,2,0:T(8,128)} %copy.150, f32[4,512,2]{1,2,0:T(2,128)S(1)} %fusion.44, f32[4,2,128,512]{3,2,1,0:T(8,128)S(1)} %fusion.33, bf16[4,512,2,128]{3,2,1,0:T(2,128)(2,1)S(1)} %copy-done.6, f32[4,2,512,512]{2,3,1,0:T(8,128)S(1)} %copy-done.3, ...), kind=kOutput, calls=%fused_computation.28 | convolution fusion | flops 3226464256 | bytes 16809984 | tf_op jit(solution)/shard_map/bhts,bshd->bthd/dot_general | solution.py:59
  185.7 5.7 %fusion.37 = f32[4,2,512,512]{2,3,1,0:T(8,128)} fusion(f32[4,512,2,128]{1,3,2,0:T(8,128)S(1)} %get-tuple-element.348, bf16[4,512,2,128]{3,2,1,0:T(2,128)(2,1)S(1)} %copy-done.6), kind=kOutput, calls=%fused_computation.56 | convolution fusion | flops 3221225472 | bytes 11534336 | tf_op jit(solution)/shard_map/bthd,bshd->bhts/dot_general | solution.py:67
  191.3 3.0 fusion.46
  196.2 10.6 %fusion.3 = f32[4,2,512,256]{3,2,1,0:T(8,128)S(1)} fusion(f32[4,2,512,512]{2,3,1,0:T(8,128)} %fusion.37, f32[4,2,512]{2,1,0:T(2,128)S(1)} %bitcast_divide_fusion, f32[512,512]{0,1:T(8,128)S(1)} %fusion.25, bf16[4,512,2,256]{3,2,1,0:T(2,128)(2,1)} %copy-done), kind=kOutput, calls=%fused_computation.9 | convolution fusion | flops 6446645248 | bytes 15745024 | tf_op jit(solution)/shard_map/bhts,bshf->bthf/dot_general | solution.py:74
  206.8 4.6 %fusion.8 = bf16[4,512,2,256]{3,1,2,0:T(8,128)(2,1)S(1)} fusion(f32[4,2,512,256]{3,2,1,0:T(8,128)S(1)} %fusion.3, f32[4,512,2,128]{1,3,2,0:T(8,128)S(1)} %copy-done.2, f32[4,2,256,128]{3,2,1,0:T(8,128)S(1)} %copy-done.11, f32[4,512,2]{1,2,0:T(2,128)S(1)} %bitcast.103, f32[4,2,256]{2,1,0:T(2,128)S(1)} %copy.157), kind=kOutput, calls=%fused_computation.18 | convolution fusion | flops 1615855616 | bytes 9461760 | tf_op jit(solution)/shard_map/bhfd,bthd->bthf/dot_general | solution.py:75
  211.5 3.5 %copy.158 = bf16[4,512,2,256]{3,2,1,0:T(2,128)(2,1)} copy(bf16[4,512,2,256]{3,1,2,0:T(8,128)(2,1)S(1)} %fusion.8) | data formatting | bytes 4194304 | tf_op jit(solution)/shard_map/convert_element_type | solution.py:80
  214.9 4.4 %all_to_all.73 = bf16[8,256,512]{2,1,0:T(8,128)(2,1)} reshape(bf16[4,512,2,256]{3,2,1,0:T(2,128)(2,1)} %copy.158) | data formatting | bytes 4194304 | tf_op jit(solution)/shard_map/all_to_all | solution.py:108
  219.3 4.4 %all-to-all-start.3 = ((bf16[8,256,512]{2,1,0:T(8,128)(2,1)}), bf16[8,256,512]{2,1,0:T(8,128)(2,1)}, u32[]{:S(2)}, u32[]{:S(2)}) async-start(bf16[8,256,512]{2,1,0:T(8,128)(2,1)} %all_to_all.73), calls=%async_computation.3 | async-start | bytes 4194304 | tf_op jit(solution)/shard_map/all_to_all | solution.py:108
  224.6 5.4 %all-gather.3 = f32[4,2,256]{2,1,0:T(2,128)S(1)} all-gather(f32[1,2,256]{2,1,0:T(2,128)S(1)} %bitcast.108), channel_id=4, replica_groups=mesh['ctx'=4,'grp'=8] {'ctx'}, dimensions={0}, use_global_device_ids=true | all-gather | bytes 10240 | tf_op jit(solution)/shard_map/all_gather | solution.py:14
  230.0 9.9 %fusion.2 = f32[4,2,512,256]{3,2,1,0:T(8,128)} fusion(f32[4,2,512,512]{2,3,1,0:T(8,128)} %fusion.37, f32[4,2,512]{2,1,0:T(2,128)S(1)} %bitcast_divide_fusion, f32[512,512]{0,1:T(8,128)S(1)} %fusion.25, bf16[4,512,2,256]{3,2,1,0:T(2,128)(2,1)S(1)} %reshape.63), kind=kOutput, calls=%fused_computation.8 | convolution fusion | flops 6446645248 | bytes 15745024 | tf_op jit(solution)/shard_map/bhts,bthf->bshf/dot_general | solution.py:77
  239.9 4.4 %while.35 = (s32[]{:T(128)}, f32[2,256,128]{2,1,0:T(8,128)S(1)}, f32[2,256]{1,0:T(2,128)S(1)}, s32[]{:T(128)}, f32[4,2,256,128]{3,2,1,0:T(8,128)}, /*index=5*/f3...) while((s32[]{:T(128)}, f32[2,256,128]{2,1,0:T(8,128)S(1)}, ...), condition=%wide.region_13.14_spmd.clone, body=%wide.region_12.13_spmd.clone.sunk | while | flops 198152 | bytes 792761 | solution.py:27
  245.5 4.3 %fusion.6 = bf16[4,512,2,256]{3,1,2,0:T(8,128)(2,1)S(1)} fusion(f32[4,2,512,256]{3,2,1,0:T(8,128)} %fusion.2, f32[4,2,256,128]{2,3,1,0:T(8,128)S(1)} %fusion.23, f32[4,2,256]{2,1,0:T(2,128)S(1)} %fusion.24, bf16[4,512,2,128]{3,2,1,0:T(2,128)(2,1)S(1)} %copy-done.7), kind=kOutput, calls=%fused_computation.15 | convolution fusion | flops 1614807040 | bytes 8396800 | tf_op jit(solution)/shard_map/bhfd,bshd->bshf/dot_general | solution.py:78
  252.1 2.6 all_to_all.77
  254.7 18.0 %all-to-all-done.3 = bf16[8,256,512]{2,1,0:T(8,128)(2,1)} async-done(((bf16[8,256,512]{2,1,0:T(8,128)(2,1)}), bf16[8,256,512]{2,1,0:T(8,128)(2,1)}, u32[]{:S(2)}, u32[]{:S(2)}) %all-to-all-start.3) | async-done | bytes 2097184 | tf_op jit(solution)/shard_map/all_to_all | solution.py:108
  272.7 3.6 %all-to-all-start.4 = ((bf16[8,256,512]{2,1,0:T(8,128)(2,1)}), bf16[8,256,512]{2,1,0:T(8,128)(2,1)S(1)}, u32[]{:S(2)}, u32[]{:S(2)}) async-start(bf16[8,256,512]{2,1,0:T(8,128)(2,1)} %all_to_all.77), calls=%async_computation.4 | async-start | bytes 4194304 | tf_op jit(solution)/shard_map/all_to_all | solution.py:109
  276.3 3.9 %copy.159 = bf16[256,8,512]{0,2,1:T(8,128)(2,1)} copy(bf16[256,8,512]{2,0,1:T(8,128)(2,1)} %bitcast.11) | data formatting | bytes 4194304 | tf_op jit(solution)/shard_map/all_to_all | solution.py:108
  280.2 4.1 %copy.169 = bf16[256,4096]{1,0:T(8,128)(2,1)} copy(bf16[256,4096]{0,1:T(8,128)(2,1)} %bitcast.95) | data formatting | bytes 4194304
  284.2 40.5 %all-to-all-done.4 = bf16[8,256,512]{2,1,0:T(8,128)(2,1)S(1)} async-done(((bf16[8,256,512]{2,1,0:T(8,128)(2,1)}), bf16[8,256,512]{2,1,0:T(8,128)(2,1)S(1)}, u32[]{:S(2)}, u32[]{:S(2)}) %all-to-all-start.4) | async-done | bytes 2097184 | tf_op jit(solution)/shard_map/all_to_all | solution.py:109
  327.1 4.1 %copy.170 = bf16[256,4096]{1,0:T(8,128)(2,1)} copy(bf16[256,4096]{0,1:T(8,128)(2,1)} %bitcast.96) | data formatting | bytes 4194304
  (84 shorter events, 40.0 us)
Async XLA Ops:
  7.2 9.7 %copy-start.14 = (bf16[256,4096]{1,0:T(8,128)(2,1)S(1)}, bf16[256,4096]{1,0:T(8,128)(2,1)}, u32[]{:S(2)}) copy-start(bf16[256,4096]{1,0:T(8,128)(2,1)} %param.9) | copy-start | bytes 6291460
  9.6 33.0 %all-to-all-start.2 = ((bf16[256,8,256]{2,0,1:T(8,128)(2,1)}), bf16[256,8,256]{2,0,1:T(8,128)(2,1)S(1)}, u32[]{:S(2)}, u32[]{:S(2)}) async-start(bf16[256,8,256]{2,0,1:T(8,128)(2,1)} %bitcast.79), calls=%async_computation.2 | async-start | bytes 2097152 | tf_op jit(solution)/shard_map/all_to_all | solution.py:92
  42.6 1.0 copy-start.12
  43.6 52.0 %all-to-all-start.1 = ((bf16[256,8,512]{2,0,1:T(8,128)(2,1)}), bf16[256,8,512]{2,0,1:T(8,128)(2,1)S(1)}, u32[]{:S(2)}, u32[]{:S(2)}) async-start(bf16[256,8,512]{2,0,1:T(8,128)(2,1)} %bitcast.94), calls=%async_computation.1 | async-start | bytes 4194304 | tf_op jit(solution)/shard_map/all_to_all | solution.py:91
  95.6 1.3 copy-start.4
  96.9 52.2 %all-to-all-start = ((bf16[256,8,512]{2,0,1:T(8,128)(2,1)}), bf16[256,8,512]{2,0,1:T(8,128)(2,1)}, u32[]{:S(2)}, u32[]{:S(2)}) async-start(bf16[256,8,512]{2,0,1:T(8,128)(2,1)} %bitcast.92), calls=%async_computation | async-start | bytes 4194304 | tf_op jit(solution)/shard_map/all_to_all | solution.py:90
  101.3 64.4 %all-gather.7.cloned.1.call-start = ((), (), s32[]{:S(2)}) async-start(), calls=%async_computation.5 | async-start | bytes 1310720 | tf_op jit(solution)/shard_map/all_gather | solution.py:14
  102.7 2.9 copy-start.5
  105.6 2.5 copy-start
  108.2 131.7 %all-gather.9.cloned.1.call-start = ((), (), s32[]{:S(2)}) async-start(), calls=%async_computation.6 | async-start | bytes 1310720 | tf_op jit(solution)/shard_map/all_gather | solution.py:14
  172.7 1.8 copy-start.8
  172.7 1.8 copy-start.13
  172.7 4.4 %copy-start.6 = (bf16[4,512,2,128]{3,2,1,0:T(2,128)(2,1)S(1)}, bf16[4,512,2,128]{3,2,1,0:T(2,128)(2,1)}, u32[]{:S(2)}) copy-start(bf16[4,512,2,128]{3,2,1,0:T(2,128)(2,1)} %copy-done.5) | copy-start | bytes 3145732
  174.5 3.8 %copy-start.3 = (f32[4,2,512,512]{2,3,1,0:T(8,128)S(1)}, f32[4,2,512,512]{2,3,1,0:T(8,128)}, u32[]{:S(2)}) copy-start(f32[4,2,512,512]{2,3,1,0:T(8,128)} %get-tuple-element.352) | copy-start | bytes 25165828
  174.7 2.4 copy-start.10
  185.7 5.7 %copy-start.1 = (f32[4,512,2,128]{1,3,2,0:T(8,128)}, f32[4,512,2,128]{1,3,2,0:T(8,128)S(1)}, u32[]{:S(2)}) copy-start(f32[4,512,2,128]{1,3,2,0:T(8,128)S(1)} %get-tuple-element.348) | copy-start | bytes 6291460
  196.2 10.6 %copy-start.2 = (f32[4,512,2,128]{1,3,2,0:T(8,128)S(1)}, f32[4,512,2,128]{1,3,2,0:T(8,128)}, u32[]{:S(2)}) copy-start(f32[4,512,2,128]{1,3,2,0:T(8,128)} %copy-done.1) | copy-start | bytes 6291460
  196.2 10.6 %copy-start.11 = (f32[4,2,256,128]{3,2,1,0:T(8,128)S(1)}, f32[4,2,256,128]{3,2,1,0:T(8,128)}, u32[]{:S(2)}) copy-start(f32[4,2,256,128]{3,2,1,0:T(8,128)} %copy-done.10) | copy-start | bytes 3145732
  219.3 53.4 %all-to-all-start.3 = ((bf16[8,256,512]{2,1,0:T(8,128)(2,1)}), bf16[8,256,512]{2,1,0:T(8,128)(2,1)}, u32[]{:S(2)}, u32[]{:S(2)}) async-start(bf16[8,256,512]{2,1,0:T(8,128)(2,1)} %all_to_all.73), calls=%async_computation.3 | async-start | bytes 4194304 | tf_op jit(solution)/shard_map/all_to_all | solution.py:108
  239.9 4.6 %copy-start.9 = (f32[4,2,256,128]{2,3,1,0:T(8,128)S(1)}, f32[4,2,256,128]{2,3,1,0:T(8,128)}, u32[]{:S(2)}) copy-start(f32[4,2,256,128]{2,3,1,0:T(8,128)} %get-tuple-element.354) | copy-start | bytes 3145732
  244.3 1.2 copy-start.7
  272.7 52.1 %all-to-all-start.4 = ((bf16[8,256,512]{2,1,0:T(8,128)(2,1)}), bf16[8,256,512]{2,1,0:T(8,128)(2,1)S(1)}, u32[]{:S(2)}, u32[]{:S(2)}) async-start(bf16[8,256,512]{2,1,0:T(8,128)(2,1)} %all_to_all.77), calls=%async_computation.4 | async-start | bytes 4194304 | tf_op jit(solution)/shard_map/all_to_all | solution.py:109
Sparse Core Ops, SparseCore 0:
  108.3 18.0 all-gather.6
  196.3 15.7 all-gather.8
where the time goes:
time: 339 us; the launch traced here: 338 us
  waiting for transfers between devices  164 us (48%)
  matrix products  59.1 us (17%)
  local copies, waits for them, and re-layouts  51.6 us (15%)
  starting transfers between devices  23.3 us (7%)
  other arithmetic  14.4 us (4%)
  between operations  14.4 us (4%)
  blocking collectives  10.8 us (3%)
    all_to_all x1, waiting for transfers between devices, on_device(): lax.all_to_all(key_feat, 'grp', split_axis=1, concat_axis=0, tiled=True)  45.3 us
    all_to_all x1, waiting for transfers between devices, on_device(): lax.all_to_all(key_head, 'grp', split_axis=0, concat_axis=1, tiled=True)  40.5 us
    all_to_all x1, waiting for transfers between devices, on_device(): lax.all_to_all(query_feat, 'grp', split_axis=1, concat_axis=0, tiled=True)  36.3 us
    all_to_all x1, waiting for transfers between devices, on_device(): lax.all_to_all(values, 'grp', split_axis=1, concat_axis=0, tiled=True)  24.2 us
    all_to_all x1, waiting for transfers between devices, on_device(): lax.all_to_all(query_head, 'grp', split_axis=0, concat_axis=1, tiled=True)  18 us
    unnamed x33, local copies, waits for them, and re-layouts  12.5 us
    select_n x16, other arithmetic, step(): return jax.tree.map(lambda a, b: jnp.where(reached, a, b), new, before)  11.3 us
    all_gather x2, blocking collectives, entering(): everything = jax.tree.map(lambda part: lax.all_gather(part, axis), array)  10.8 us
  transfers between devices with their start and end apart: 7, of which 5 were waited for; matrix products, arithmetic and copies ran while one was open for 22% of the time, Pallas kernels for 0%

commit v1 on v0

v1 whole, which is shorter than its diff:
```python
import functools
import math

import jax
import jax.numpy as jnp
from jax import lax
from jax.experimental import pallas as pl
from jax.experimental.pallas import tpu as pltpu
from jax.sharding import PartitionSpec as P

H = 16
SIDE = 16
SPAN = 125.0
F32 = jnp.float32
BF16 = jnp.bfloat16


def dot(a, b, dims):
    return lax.dot_general(a, b, (dims, ((), ())), preferred_element_type=F32)


NN = ((1,), (0,))
NT = ((1,), (1,))
TN = ((0,), (0,))


def split(x):
    hi = x.astype(BF16)
    return hi, (x - hi.astype(F32)).astype(BF16)


def encode(x):
    scale = (jnp.maximum(jnp.max(jnp.abs(x), axis=0, keepdims=True), 1e-20) * 1.01).astype(BF16)
    y = jnp.exp2(jnp.abs(x) * (2 * SPAN / scale.astype(F32)) - SPAN)
    return jnp.where(x < 0, -y, y).astype(BF16), scale


def decode(code, scale):
    y = code.astype(F32)
    x = (jnp.log2(jnp.abs(y)) + SPAN) * (scale.astype(F32) * (0.5 / SPAN))
    return jnp.where(y < 0, -x, x)


def side_rows(scale, row2):
    hi = row2.astype(BF16).astype(F32)
    mid = (row2 - hi).astype(BF16).astype(F32)
    low = row2 - hi - mid
    pad = jnp.zeros((SIDE - 7, row2.shape[1]), F32)
    return jnp.concatenate([scale.astype(F32), hi, mid, low, pad], axis=0).astype(BF16)


def read_side(side):
    s = side.astype(F32)
    return s[0:1], s[1:3] + s[3:5] + s[5:7]


def write_state(out_ref, state, row):
    pieces, rows = out_ref.shape[0], out_ref.shape[1] - SIDE
    code, scale = encode(state)
    width = state.shape[1]
    row2 = jnp.concatenate([row[:, :width], row[:, width:]], axis=0)
    side = side_rows(scale, row2)
    for p in range(pieces):
        out_ref[p, :rows, :] = code[p * rows : (p + 1) * rows]
        out_ref[p, rows:, :] = side


def read_state(ref):
    pieces, rows = ref.shape[0], ref.shape[1] - SIDE
    parts = []
    for p in range(pieces):
        scale, row2 = read_side(ref[p, rows:, :])
        parts.append(decode(ref[p, :rows, :], scale))
    row = jnp.concatenate([row2[0:1], row2[1:2]], axis=1)
    return jnp.concatenate(parts, axis=0), row


def local_kernel(k_ref, v_ref, out_ref):
    k = k_ref[...]
    write_state(out_ref, dot(k, v_ref[...], TN), jnp.sum(k.astype(F32), axis=0, keepdims=True))


def scan_kernel(reverse, in_ref, out_ref):
    n, rows = in_ref.shape[0], in_ref.shape[1] - SIDE

    def step(i, carry):
        state, row2 = carry
        d = n - 1 - i if reverse else i
        code, scale = encode(state)
        out_ref[d, :rows, :] = code
        out_ref[d, rows:, :] = side_rows(scale, row2)
        scale_in, row_in = read_side(in_ref[d, rows:, :])
        return state + decode(in_ref[d, :rows, :], scale_in), row2 + row_in

    width = in_ref.shape[2]
    lax.fori_loop(0, n, step, (jnp.zeros((rows, width), F32), jnp.zeros((2, width), F32)))


def forward_kernel(scale, q_ref, k_ref, v_ref, t_ref, before_ref, qg_ref, kl_ref, adj_ref):
    q, k, v = q_ref[...], k_ref[...], v_ref[...]
    kv, key_row = read_state(before_ref)
    kv_hi, kv_lo = split(kv)
    rows = q.shape[0]
    causal = lax.broadcasted_iota(jnp.int32, (rows, rows), 1) <= lax.broadcasted_iota(
        jnp.int32, (rows, rows), 0
    )
    q_wide = q.astype(F32)
    scores = jnp.where(causal, dot(q, k, NT), 0.0)
    s_hi, s_lo = split(scores)
    numer = dot(s_hi, v, NN) + dot(s_lo, v, NN) + dot(q, kv_hi, NN) + dot(q, kv_lo, NN)
    denom = jnp.sum(scores, axis=1, keepdims=True) + jnp.sum(q_wide * key_row, axis=1, keepdims=True)
    inv = 1.0 / denom
    student = numer * inv
    resid = student - t_ref[...].astype(F32)
    d_numer = resid * inv
    d_denom = -jnp.sum(resid * student, axis=1, keepdims=True) * inv
    dn_hi, dn_lo = split(d_numer)
    adj = dot(q, dn_hi, TN) + dot(q, dn_lo, TN)
    write_state(adj_ref, adj, jnp.sum(d_denom * q_wide, axis=0, keepdims=True))
    mixed = jnp.where(causal, dot(dn_hi, v, NT) + dot(dn_lo, v, NT) + d_denom, 0.0)
    m_hi, m_lo = split(mixed)
    q_grad = dot(m_hi, k, NN) + dot(m_lo, k, NN)
    q_grad = q_grad + dot(dn_hi, kv_hi, NT) + dot(dn_hi, kv_lo, NT) + dot(dn_lo, kv_hi, NT)
    q_grad = q_grad + d_denom * key_row
    qg_ref[...] = (scale * q_grad).astype(BF16)
    kl_ref[...] = dot(m_hi, q, TN) + dot(m_lo, q, TN)


def backward_kernel(scale, v_ref, kl_ref, after_ref, kg_ref):
    adj, row = read_state(after_ref)
    a_hi, a_lo = split(adj)
    v = v_ref[...]
    k_grad = kl_ref[...] + dot(v, a_hi, NT) + dot(v, a_lo, NT) + row
    kg_ref[...] = (scale * k_grad).astype(BF16)


def on_device(n, query_feat, key_feat, values, teacher):
    rows = query_feat.shape[0]
    feat = query_feat.shape[1] // H
    width = values.shape[1] // H
    scale = float(rows * n) ** 0.5
    share = H * feat // n
    per_head = feat // share
    everyone = ("ctx", "grp")
    params = pltpu.CompilerParams(vmem_limit_bytes=32 * 1024 * 1024)

    def cols(w):
        return pl.BlockSpec((rows, w), lambda h: (0, h))

    state_spec = pl.BlockSpec((per_head, share + SIDE, width), lambda h: (h, 0, 0))
    state_shape = jax.ShapeDtypeStruct((n, share + SIDE, width), BF16)

    def swap(x):
        return lax.all_to_all(x, everyone, split_axis=0, concat_axis=0, tiled=True)

    def scan(x, reverse):
        return pl.pallas_call(
            functools.partial(scan_kernel, reverse),
            out_shape=state_shape,
            compiler_params=params,
            name="scan",
        )(x)

    local = pl.pallas_call(
        local_kernel,
        grid=(H,),
        in_specs=[cols(feat), cols(width)],
        out_specs=state_spec,
        out_shape=state_shape,
        compiler_params=params,
        name="local_state",
    )(key_feat, values)
    before = swap(scan(swap(local), False))
    target = lax.all_to_all(teacher, "grp", split_axis=0, concat_axis=1, tiled=True)
    query_grad, key_local, adj = pl.pallas_call(
        functools.partial(forward_kernel, scale),
        grid=(H,),
        in_specs=[cols(feat), cols(feat), cols(width), cols(width), state_spec],
        out_specs=[cols(feat), cols(feat), state_spec],
        out_shape=[
            jax.ShapeDtypeStruct((rows, H * feat), BF16),
            jax.ShapeDtypeStruct((rows, H * feat), F32),
            state_shape,
        ],
        compiler_params=params,
        name="forward",
    )(query_feat, key_feat, values, target, before)
    after = swap(scan(swap(adj), True))
    key_grad = pl.pallas_call(
        functools.partial(backward_kernel, scale),
        grid=(H,),
        in_specs=[cols(width), cols(feat), state_spec],
        out_specs=cols(feat),
        out_shape=jax.ShapeDtypeStruct((rows, H * feat), BF16),
        compiler_params=params,
        name="backward",
    )(values, key_local, after)
    return query_grad, key_grad


def solution(mesh):
    placed = (
        P(("ctx", "grp"), None),
        P(("ctx", "grp"), None),
        P(("ctx", "grp"), None),
        P("ctx", "grp"),
    )
    return jax.shard_map(
        functools.partial(on_device, math.prod(mesh.shape.values())),
        mesh=mesh,
        in_specs=placed,
        out_specs=(P(("ctx", "grp"), None), P(("ctx", "grp"), None)),
        check_vma=False,
    )
```

time: 339 us -> 212 us (0.63)
  waiting for transfers between devices: 164 us -> 51.5 us
  blocking collectives: 10.8 us -> 102 us
  matrix products: 59.1 us -> 0 us
  local copies, waits for them, and re-layouts: 51.6 us -> 9.06 us
  Pallas kernels: 0 us -> 39.7 us
  starting transfers between devices: 23.3 us -> 7.75 us
  other arithmetic: 14.4 us -> 0 us
  between operations: 14.4 us -> 0.7 us
    all_to_all x5 -> x2, waiting for transfers between devices: 164 us -> 51.5 us  [the longest x1 28 us: swap(): return lax.all_to_all(x, everyone, split_axis=0, concat_axis=0, tiled=True)]
    all_to_all x0 -> x3, blocking collectives: none -> 102 us  [swap(): return lax.all_to_all(x, everyone, split_axis=0, concat_axis=0, tiled=True)]
    dot_general x12 -> x0, matrix products: 59.1 us -> none  [the longest x1 10.6 us: local_grads(): q_grad = jnp.einsum('bhts,bshf->bthf', mixed, fk_wide, precision=HIGH)]
    pallas_call x0 -> x5, Pallas kernels: none -> 39.7 us  [the longest x1 23.5 us: on_device(): pl.pallas_call(functools.partial(forward_kernel, scale), grid=(H,), in_sp...]
    all_to_all x7 -> x1, local copies, waits for them, and re-layouts: 20.3 us -> 2.41 us  [on_device(): lax.all_to_all(teacher, 'grp', split_axis=0, concat_axis=1, tiled=True)]
    all_to_all x5 -> x2, starting transfers between devices: 23.2 us -> 7.75 us  [the longest x1 4.25 us: on_device(): lax.all_to_all(teacher, 'grp', split_axis=0, concat_axis=1, tiled=True)]
    select_n x16 -> x0, other arithmetic: 11.3 us -> none  [step(): return jax.tree.map(lambda a, b: jnp.where(reached, a, b), new, before)]
    all_gather x2 -> x0, blocking collectives: 10.8 us -> none  [entering(): everything = jax.tree.map(lambda part: lax.all_gather(part, axis), array)]
  transfers between devices with their start and end apart: 7 -> 2, of which waited for: 5 -> 2; matrix products, arithmetic and copies ran while one was open for 22% -> 1% of each run, Pallas kernels for 0% -> 1%
where the time goes in v1:
time: 212 us; the launch traced here: 211 us
  blocking collectives  102 us (48%)
  waiting for transfers between devices  51.5 us (24%)
  Pallas kernels  39.7 us (19%)
  local copies, waits for them, and re-layouts  9.06 us (4%)
  starting transfers between devices  7.75 us (4%)
    all_to_all x3, blocking collectives, swap(): return lax.all_to_all(x, everyone, split_axis=0, concat_axis=0, tiled=True)  102 us
    all_to_all x1, waiting for transfers between devices, swap(): return lax.all_to_all(x, everyone, split_axis=0, concat_axis=0, tiled=True)  28 us
    pallas_call x1, Pallas kernels, on_device(): pl.pallas_call(functools.partial(forward_kernel, scale), grid=(H,), in_sp...  23.5 us
    all_to_all x1, waiting for transfers between devices, on_device(): lax.all_to_all(teacher, 'grp', split_axis=0, concat_axis=1, tiled=True)  23.5 us
    pallas_call x1, Pallas kernels, on_device(): pl.pallas_call(functools.partial(backward_kernel, scale), grid=(H,), in_s...  7.92 us
    unnamed x14, local copies, waits for them, and re-layouts  6.64 us
    pallas_call x1, Pallas kernels, on_device(): pl.pallas_call(local_kernel, grid=(H,), in_specs=[cols(feat), cols(width)...  5.23 us
    all_to_all x1, starting transfers between devices, on_device(): lax.all_to_all(teacher, 'grp', split_axis=0, concat_axis=1, tiled=True)  4.25 us
  transfers between devices with their start and end apart: 2, of which 2 were waited for; matrix products, arithmetic and copies ran while one was open for 1% of the time, Pallas kernels for 1%

profile of v1, /device:TPU:0, one launch (start us, length us, event | category | flops | bytes accessed | tf_op | source)
XLA Modules:
  0.0 211.1 jit_solution(1819273572337810267)
XLA Ops:
  0.6 0.0 copy-start
  0.6 1.2 copy-done
  1.9 0.0 copy-start.2
  1.9 1.6 copy-done.2
  3.4 5.2 %local_state.1 = bf16[32,144,128]{2,1,0:T(8,128)(2,1)S(1)} custom-call(bf16[256,4096]{1,0:T(8,128)(2,1)S(1)} %copy-done.2, bf16[256,2048]{1,0:T(8,128)(2,1)S(1)} %copy-done), custom_call_target="tpu_custom_call" | custom-call | tf_op jit(solution)/shard_map/local_state/pallas_call | solution.py:164
  8.7 37.5 %all_to_all.39.in_ref = bf16[32,144,128]{2,1,0:T(8,128)(2,1)S(1)} all-to-all(bf16[32,144,128]{2,1,0:T(8,128)(2,1)S(1)} %local_state.1), channel_id=1, replica_groups=mesh['ctx'=4,'grp'=8] {'ctx','grp'}, dimensions={0} | all-to-all | bytes 2359296 | tf_op jit(solution)/shard_map/all_to_all | solution.py:154
  46.2 4.2 %all-to-all-start = ((bf16[8,256,256]{2,1,0:T(8,128)(2,1)}), bf16[8,256,256]{2,1,0:T(8,128)(2,1)}, u32[]{:S(2)}, u32[]{:S(2)}) async-start(bf16[8,256,256]{2,1,0:T(8,128)(2,1)} %bitcast), calls=%async_computation | async-start | bytes 2097152 | tf_op jit(solution)/shard_map/all_to_all | solution.py:174
  50.4 1.5 scan.2
  52.0 0.0 copy-start.4
  52.0 1.0 copy-done.4
  53.0 23.5 %all-to-all-done = bf16[8,256,256]{2,1,0:T(8,128)(2,1)} async-done(((bf16[8,256,256]{2,1,0:T(8,128)(2,1)}), bf16[8,256,256]{2,1,0:T(8,128)(2,1)}, u32[]{:S(2)}, u32[]{:S(2)}) %all-to-all-start) | async-done | bytes 1048608 | tf_op jit(solution)/shard_map/all_to_all | solution.py:174
  76.5 0.0 copy-start.3
  76.5 3.5 %all-to-all-start.2 = ((bf16[32,144,128]{2,1,0:T(8,128)(2,1)}), bf16[32,144,128]{2,1,0:T(8,128)(2,1)}, u32[]{:S(2)}, u32[]{:S(2)}) async-start(bf16[32,144,128]{2,1,0:T(8,128)(2,1)} %copy-done.4), calls=%async_computation.2 | async-start | bytes 2359296 | tf_op jit(solution)/shard_map/all_to_all | solution.py:154
  80.0 0.0 copy-start.1
  80.0 2.4 %copy.8 = bf16[8,32,8,256]{3,2,0,1:T(8,128)(2,1)} copy(bf16[8,32,8,256]{3,2,1,0:T(8,128)(2,1)} %bitcast.2) | data formatting | bytes 2097152 | tf_op jit(solution)/shard_map/all_to_all | solution.py:174
  82.4 28.0 %all-to-all-done.2.before_ref = bf16[32,144,128]{2,1,0:T(8,128)(2,1)} async-done(((bf16[32,144,128]{2,1,0:T(8,128)(2,1)}), bf16[32,144,128]{2,1,0:T(8,128)(2,1)}, u32[]{:S(2)}, u32[]{:S(2)}) %all-to-all-start.2) | async-done | bytes 1179680 | tf_op jit(solution)/shard_map/all_to_all | solution.py:154
  110.4 0.0 copy-done.3
  110.4 0.0 copy-done.1
  110.4 0.0 copy-start.5
  110.4 1.2 copy-done.5
  111.6 0.0 copy-start.6
  111.6 1.6 copy-done.6
  113.2 23.5 %forward.1 = (bf16[256,4096]{1,0:T(8,128)(2,1)}, f32[256,4096]{1,0:T(8,128)S(1)}, bf16[32,144,128]{2,1,0:T(8,128)(2,1)S(1)}) custom-call(bf16[256,4096]{1,0:T(8,128)(2,1)S(1)} %copy-done.6, bf16[256,4096]{1,0:T(8,128)(2,1)S(1)} %copy-done.3, bf16[256,2048]{1,0:T(8,128)(2,1)S(1)} %copy-done.1, bf16[256,2048]{1,0:T(8,128)(2,1)S(1)} %bitcast.4, ...), custom_call_target="tpu_custom_call" | custom-call | tf_op jit(solution)/shard_map/forward/pallas_call | solution.py:175
  136.7 32.5 %all_to_all.40.in_ref = bf16[32,144,128]{2,1,0:T(8,128)(2,1)S(1)} all-to-all(bf16[32,144,128]{2,1,0:T(8,128)(2,1)S(1)} %get-tuple-element.7), channel_id=1, replica_groups=mesh['ctx'=4,'grp'=8] {'ctx','grp'}, dimensions={0} | all-to-all | bytes 2359296 | tf_op jit(solution)/shard_map/all_to_all | solution.py:154
  169.2 1.5 scan.3
  170.7 32.5 %all_to_all.41.after_ref = bf16[32,144,128]{2,1,0:T(8,128)(2,1)S(1)} all-to-all(bf16[32,144,128]{2,1,0:T(8,128)(2,1)S(1)} %scan.3), channel_id=1, replica_groups=mesh['ctx'=4,'grp'=8] {'ctx','grp'}, dimensions={0} | all-to-all | bytes 2359296 | tf_op jit(solution)/shard_map/all_to_all | solution.py:154
  203.2 7.9 %backward.1 = bf16[256,4096]{1,0:T(8,128)(2,1)} custom-call(bf16[256,2048]{1,0:T(8,128)(2,1)S(1)} %copy-done.1, f32[256,4096]{1,0:T(8,128)S(1)} %get-tuple-element.6.kl_ref, bf16[32,144,128]{2,1,0:T(8,128)(2,1)S(1)} %all_to_all.41.after_ref), custom_call_target="tpu_custom_call" | custom-call | tf_op jit(solution)/shard_map/backward/pallas_call | solution.py:189
Async XLA Ops:
  0.6 1.2 copy-start
  1.9 1.6 copy-start.2
  46.2 30.3 %all-to-all-start = ((bf16[8,256,256]{2,1,0:T(8,128)(2,1)}), bf16[8,256,256]{2,1,0:T(8,128)(2,1)}, u32[]{:S(2)}, u32[]{:S(2)}) async-start(bf16[8,256,256]{2,1,0:T(8,128)(2,1)} %bitcast), calls=%async_computation | async-start | bytes 2097152 | tf_op jit(solution)/shard_map/all_to_all | solution.py:174
  52.0 1.0 copy-start.4
  76.5 33.9 %copy-start.3 = (bf16[256,4096]{1,0:T(8,128)(2,1)S(1)}, bf16[256,4096]{1,0:T(8,128)(2,1)}, u32[]{:S(2)}) copy-start(bf16[256,4096]{1,0:T(8,128)(2,1)} %k_ref.3) | copy-start | bytes 6291460
  76.5 33.9 %all-to-all-start.2 = ((bf16[32,144,128]{2,1,0:T(8,128)(2,1)}), bf16[32,144,128]{2,1,0:T(8,128)(2,1)}, u32[]{:S(2)}, u32[]{:S(2)}) async-start(bf16[32,144,128]{2,1,0:T(8,128)(2,1)} %copy-done.4), calls=%async_computation.2 | async-start | bytes 2359296 | tf_op jit(solution)/shard_map/all_to_all | solution.py:154
  80.0 30.4 %copy-start.1 = (bf16[256,2048]{1,0:T(8,128)(2,1)S(1)}, bf16[256,2048]{1,0:T(8,128)(2,1)}, u32[]{:S(2)}) copy-start(bf16[256,2048]{1,0:T(8,128)(2,1)} %v_ref.5) | copy-start | bytes 3145732
  110.4 1.2 copy-start.5
  111.6 1.6 copy-start.6

commit v2 on v1

--- a/solution.py
+++ b/solution.py
@@ -1,5 +1,4 @@
 import functools
-import math
 
 import jax
 import jax.numpy as jnp
@@ -80,20 +79,209 @@
     write_state(out_ref, dot(k, v_ref[...], TN), jnp.sum(k.astype(F32), axis=0, keepdims=True))
 
 
-def scan_kernel(reverse, in_ref, out_ref):
-    n, rows = in_ref.shape[0], in_ref.shape[1] - SIDE
-
-    def step(i, carry):
-        state, row2 = carry
-        d = n - 1 - i if reverse else i
+def exchange_kernel(reverse, spans, depth, *refs):
+    if reverse:
+        in_ref, out_ref = refs[:2]
+        scratch = refs[2:]
+        teacher_ref = target_ref = None
+    else:
+        in_ref, teacher_ref, out_ref, target_ref = refs[:4]
+        scratch = refs[4:]
+    (stage, back, up_out, up_in, down_out, down_in, total, above, below, total_row, above_row,
+     below_row, a_send, a_recv, b_send, b_recv, u_send, u_recv, d_send, d_recv, *more) = scratch
+    plane = 2 * spans
+    chunks, rows = stage.shape[0], stage.shape[2] - SIDE
+    ctx, grp = lax.axis_index("ctx"), lax.axis_index("grp")
+    groups = 2 * depth
+    level, side_x = grp // 2, grp % 2
+    mine = ctx * 2 + side_x
+
+    def plane_peer(q):
+        return (q // 2, level * 2 + q % 2)
+
+    def remote(src, dst, send, recv, to):
+        return pltpu.make_async_remote_copy(
+            src_ref=src, dst_ref=dst, send_sem=send, recv_sem=recv, device_id=to,
+            device_id_type=pl.DeviceIdType.MESH,
+        )
+
+    barrier = pltpu.get_barrier_semaphore()
+
+    def greet(to):
+        pl.semaphore_signal(barrier, inc=1, device_id=to, device_id_type=pl.DeviceIdType.MESH)
+
+    for d in range(1, plane):
+        greet(plane_peer((mine + d) % plane))
+    for d in range(1, groups):
+        greet((ctx, (grp + d) % groups))
+    pl.semaphore_wait(barrier, plane + groups - 2)
+
+    def gather(j, d):
+        peer = (mine + d) % plane
+        return remote(in_ref.at[peer * chunks + j], stage.at[j, mine], a_send.at[j, d - 1],
+                      a_recv.at[j, d - 1], plane_peer(peer))
+
+    def scatter(j, d):
+        peer = (mine + d) % plane
+        return remote(back.at[j, peer], out_ref.at[mine * chunks + j], b_send.at[j, d - 1],
+                      b_recv.at[j, d - 1], plane_peer(peer))
+
+    def upward(j):
+        return remote(up_out.at[j], up_in.at[j], u_send.at[j], u_recv.at[j], (ctx, grp + 2))
+
+    def downward(j):
+        return remote(down_out.at[j], down_in.at[j], d_send.at[j], d_recv.at[j], (ctx, grp - 2))
+
+    for j in range(chunks):
+        for d in range(1, plane):
+            gather(j, d).start()
+    moves = []
+    if teacher_ref is not None:
+        t_send, t_recv, t_own = more
+        tokens = target_ref.shape[1]
+        for d in range(1, groups):
+            peer = (grp + d) % groups
+            moves.append(remote(teacher_ref.at[pl.ds(peer * tokens, tokens)], target_ref.at[grp],
+                                t_send.at[d - 1], t_recv.at[d - 1], (ctx, peer)))
+        for move in moves:
+            move.start()
+        own = pltpu.make_async_copy(teacher_ref.at[pl.ds(grp * tokens, tokens)], target_ref.at[grp], t_own)
+        own.start()
+    for j in range(chunks):
+        stage[j, mine] = in_ref[mine * chunks + j]
+
+    def load(ref, j, k):
+        scale, row2 = read_side(ref[j, k, rows:, :])
+        return decode(ref[j, k, :rows, :], scale), row2
+
+    def store(ref, j, k, state, row2):
         code, scale = encode(state)
-        out_ref[d, :rows, :] = code
-        out_ref[d, rows:, :] = side_rows(scale, row2)
-        scale_in, row_in = read_side(in_ref[d, rows:, :])
-        return state + decode(in_ref[d, :rows, :], scale_in), row2 + row_in
-
-    width = in_ref.shape[2]
-    lax.fori_loop(0, n, step, (jnp.zeros((rows, width), F32), jnp.zeros((2, width), F32)))
+        ref[j, k, :rows, :] = code
+        ref[j, k, rows:, :] = side_rows(scale, row2)
+
+    def chain(j, has_in, has_out, copy, in_buf, out_buf, kept, kept_row):
+        @pl.when(has_in)
+        def _():
+            copy(j).wait_recv()
+            for k in range(spans):
+                state, row2 = load(in_buf, j, k)
+                kept[j, k] = state
+                kept_row[j, k] = row2
+
+        @pl.when(jnp.logical_not(has_in))
+        def _():
+            for k in range(spans):
+                kept[j, k] = jnp.zeros_like(kept[j, k])
+                kept_row[j, k] = jnp.zeros_like(kept_row[j, k])
+
+        @pl.when(has_out)
+        def _():
+            for k in range(spans):
+                store(out_buf, j, k, kept[j, k] + total[j, k], kept_row[j, k] + total_row[j, k])
+            copy(j).start()
+
+    def step(t, unused):
+        @pl.when(t < chunks)
+        def _():
+            for d in range(1, plane):
+                gather(t, d).wait_recv()
+            for k in range(spans):
+                first, first_row = load(stage, t, 2 * k)
+                second, second_row = load(stage, t, 2 * k + 1)
+                total[t, k] = first + second
+                total_row[t, k] = first_row + second_row
+
+        j_up = t - level
+
+        @pl.when((j_up >= 0) & (j_up < chunks))
+        def _():
+            chain(j_up, level > 0, level < depth - 1, upward, up_in, up_out, below, below_row)
+
+        j_down = t - (depth - 1 - level)
+
+        @pl.when((j_down >= 0) & (j_down < chunks))
+        def _():
+            chain(j_down, level < depth - 1, level > 0, downward, down_in, down_out, above, above_row)
+
+        j_end = t - (depth - 1)
+
+        @pl.when(j_end >= 0)
+        def _():
+            j = j_end
+            run = jnp.zeros(total.shape[2:], F32)
+            run_row = jnp.zeros(total_row.shape[2:], F32)
+            for i in range(spans):
+                k = spans - 1 - i if reverse else i
+                near, near_row = (above, above_row) if reverse else (below, below_row)
+                state, row2 = run + near[j, k], run_row + near_row[j, k]
+                one, two = (2 * k + 1, 2 * k) if reverse else (2 * k, 2 * k + 1)
+                store(back, j, one, state, row2)
+                beside, beside_row = load(stage, j, one)
+                store(back, j, two, state + beside, row2 + beside_row)
+                run = run + below[j, k] + total[j, k] + above[j, k]
+                run_row = run_row + below_row[j, k] + total_row[j, k] + above_row[j, k]
+            for d in range(1, plane):
+                scatter(j, d).start()
+            out_ref[mine * chunks + j] = back[j, mine]
+
+        return unused
+
+    lax.fori_loop(0, chunks + depth - 1, step, 0)
+
+    for j in range(chunks):
+        for d in range(1, plane):
+            gather(j, d).wait_send()
+            scatter(j, d).wait()
+
+    @pl.when(level < depth - 1)
+    def _():
+        for j in range(chunks):
+            upward(j).wait_send()
+
+    @pl.when(level > 0)
+    def _():
+        for j in range(chunks):
+            downward(j).wait_send()
+
+    if teacher_ref is not None:
+        for move in moves:
+            move.wait()
+        own.wait()
+
+
+def exchange(reverse, spans, depth, pieces, teacher=None):
+    count, length, width = pieces.shape
+    plane, groups = 2 * spans, 2 * depth
+    chunks = count // plane
+    vmem = pl.BlockSpec(memory_space=pltpu.VMEM)
+    anywhere = pl.BlockSpec(memory_space=pl.ANY)
+    in_specs, out_specs, args = [vmem], [vmem], [pieces]
+    out_shape = [jax.ShapeDtypeStruct(pieces.shape, BF16)]
+    dma = pltpu.SemaphoreType.DMA
+    line = pltpu.VMEM((chunks, spans, length, width), BF16)
+    wide = pltpu.VMEM((chunks, spans, length - SIDE, width), F32)
+    row = pltpu.VMEM((chunks, spans, 2, width), F32)
+    block = pltpu.VMEM((chunks, plane, length, width), BF16)
+    scratch = [block, block, line, line, line, line, wide, wide, wide, row, row, row]
+    scratch += [dma((chunks, plane - 1))] * 4 + [dma((chunks,))] * 4
+    if teacher is not None:
+        in_specs.append(anywhere)
+        out_specs.append(anywhere)
+        args.append(teacher)
+        shape = (groups, teacher.shape[0] // groups, teacher.shape[1])
+        out_shape.append(jax.ShapeDtypeStruct(shape, BF16))
+        scratch += [dma((groups - 1,)), dma((groups - 1,)), dma]
+    return pl.pallas_call(
+        functools.partial(exchange_kernel, reverse, spans, depth),
+        in_specs=in_specs,
+        out_specs=out_specs,
+        out_shape=out_shape,
+        scratch_shapes=scratch,
+        compiler_params=pltpu.CompilerParams(
+            collective_id=1 if reverse else 0, has_side_effects=True, vmem_limit_bytes=56 * 1024 * 1024
+        ),
+        name="suffix_exchange" if reverse else "prefix_exchange",
+    )(*args)
 
 
 def forward_kernel(scale, q_ref, k_ref, v_ref, t_ref, before_ref, qg_ref, kl_ref, adj_ref):
@@ -111,7 +299,7 @@
     denom = jnp.sum(scores, axis=1, keepdims=True) + jnp.sum(q_wide * key_row, axis=1, keepdims=True)
     inv = 1.0 / denom
     student = numer * inv
-    resid = student - t_ref[...].astype(F32)
+    resid = student - t_ref[0].astype(F32)
     d_numer = resid * inv
     d_denom = -jnp.sum(resid * student, axis=1, keepdims=True) * inv
     dn_hi, dn_lo = split(d_numer)
@@ -134,32 +322,22 @@
     kg_ref[...] = (scale * k_grad).astype(BF16)
 
 
-def on_device(n, query_feat, key_feat, values, teacher):
+def on_device(spans, groups, query_feat, key_feat, values, teacher):
     rows = query_feat.shape[0]
     feat = query_feat.shape[1] // H
     width = values.shape[1] // H
-    scale = float(rows * n) ** 0.5
-    share = H * feat // n
-    per_head = feat // share
-    everyone = ("ctx", "grp")
-    params = pltpu.CompilerParams(vmem_limit_bytes=32 * 1024 * 1024)
+    scale = float(rows * spans * groups) ** 0.5
+    depth = groups // 2
+    per_head = feat // width
+    per_group = H // groups
+    params = pltpu.CompilerParams(vmem_limit_bytes=56 * 1024 * 1024)
 
     def cols(w):
         return pl.BlockSpec((rows, w), lambda h: (0, h))
 
-    state_spec = pl.BlockSpec((per_head, share + SIDE, width), lambda h: (h, 0, 0))
-    state_shape = jax.ShapeDtypeStruct((n, share + SIDE, width), BF16)
-
-    def swap(x):
-        return lax.all_to_all(x, everyone, split_axis=0, concat_axis=0, tiled=True)
-
-    def scan(x, reverse):
-        return pl.pallas_call(
-            functools.partial(scan_kernel, reverse),
-            out_shape=state_shape,
-            compiler_params=params,
-            name="scan",
-        )(x)
+    state_spec = pl.BlockSpec((per_head, width + SIDE, width), lambda h: (h, 0, 0))
+    state_shape = jax.ShapeDtypeStruct((H * per_head, width + SIDE, width), BF16)
+    target_spec = pl.BlockSpec((1, rows, width), lambda h: (h // per_group, 0, h % per_group))
 
     local = pl.pallas_call(
         local_kernel,
@@ -170,12 +348,11 @@
         compiler_params=params,
         name="local_state",
     )(key_feat, values)
-    before = swap(scan(swap(local), False))
-    target = lax.all_to_all(teacher, "grp", split_axis=0, concat_axis=1, tiled=True)
+    before, target = exchange(False, spans, depth, local, teacher)
     query_grad, key_local, adj = pl.pallas_call(
         functools.partial(forward_kernel, scale),
         grid=(H,),
-        in_specs=[cols(feat), cols(feat), cols(width), cols(width), state_spec],
+        in_specs=[cols(feat), cols(feat), cols(width), target_spec, state_spec],
         out_specs=[cols(feat), cols(feat), state_spec],
         out_shape=[
             jax.ShapeDtypeStruct((rows, H * feat), BF16),
@@ -185,7 +362,7 @@
         compiler_params=params,
         name="forward",
     )(query_feat, key_feat, values, target, before)
-    after = swap(scan(swap(adj), True))
+    (after,) = exchange(True, spans, depth, adj)
     key_grad = pl.pallas_call(
         functools.partial(backward_kernel, scale),
         grid=(H,),
@@ -206,7 +383,7 @@
         P("ctx", "grp"),
     )
     return jax.shard_map(
-        functools.partial(on_device, math.prod(mesh.shape.values())),
+        functools.partial(on_device, mesh.shape["ctx"], mesh.shape["grp"]),
         mesh=mesh,
         in_specs=placed,
         out_specs=(P(("ctx", "grp"), None), P(("ctx", "grp"), None)),

time: 212 us -> 154 us (0.73)
  Pallas kernels: 39.7 us -> 152 us
  blocking collectives: 102 us -> 0 us
  waiting for transfers between devices: 51.5 us -> 0 us
  local copies, waits for them, and re-layouts: 9.06 us -> 0 us
  starting transfers between devices: 7.75 us -> 0 us
    pallas_call x2, Pallas kernels: 3.01 us -> 106 us  [exchange(): pl.pallas_call(functools.partial(exchange_kernel, reverse, spans, depth),...]
    all_to_all x3 -> x0, blocking collectives: 102 us -> none  [swap(): return lax.all_to_all(x, everyone, split_axis=0, concat_axis=0, tiled=True)]
    all_to_all x2 -> x0, waiting for transfers between devices: 51.5 us -> none  [the longest x1 28 us: swap(): return lax.all_to_all(x, everyone, split_axis=0, concat_axis=0, tiled=True)]
    all_to_all x2 -> x0, starting transfers between devices: 7.75 us -> none  [the longest x1 4.25 us: on_device(): lax.all_to_all(teacher, 'grp', split_axis=0, concat_axis=1, tiled=True)]
    unnamed x14 -> x0, local copies, waits for them, and re-layouts: 6.64 us -> none
    pallas_call x1, Pallas kernels: 5.23 us -> 11.2 us  [on_device(): pl.pallas_call(local_kernel, grid=(H,), in_specs=[cols(feat), cols(width)...]
    pallas_call x1, Pallas kernels: 7.92 us -> 11.9 us  [on_device(): pl.pallas_call(functools.partial(backward_kernel, scale), grid=(H,), in_s...]
    all_to_all x1 -> x0, local copies, waits for them, and re-layouts: 2.41 us -> none  [on_device(): lax.all_to_all(teacher, 'grp', split_axis=0, concat_axis=1, tiled=True)]
  transfers between devices with their start and end apart: 2 -> 0, of which waited for: 2 -> 0; matrix products, arithmetic and copies ran while one was open for 1% -> 0% of each run, Pallas kernels for 1% -> 0%
where the time goes in v2:
time: 154 us; the launch traced here: 153 us
  Pallas kernels  152 us (99%)
    pallas_call x2, Pallas kernels, exchange(): pl.pallas_call(functools.partial(exchange_kernel, reverse, spans, depth),...  106 us
    pallas_call x1, Pallas kernels, on_device(): pl.pallas_call(functools.partial(forward_kernel, scale), grid=(H,), in_sp...  23.1 us
    pallas_call x1, Pallas kernels, on_device(): pl.pallas_call(functools.partial(backward_kernel, scale), grid=(H,), in_s...  11.9 us
    pallas_call x1, Pallas kernels, on_device(): pl.pallas_call(local_kernel, grid=(H,), in_specs=[cols(feat), cols(width)...  11.2 us

profile of v2, /device:TPU:0, one launch (start us, length us, event | category | flops | bytes accessed | tf_op | source)
XLA Modules:
  0.0 152.8 jit_solution(9027113609397777037)
XLA Ops:
  0.6 11.2 %local_state.1.refs_0_ = bf16[32,144,128]{2,1,0:T(8,128)(2,1)} custom-call(bf16[256,4096]{1,0:T(8,128)(2,1)} %k_ref.3, bf16[256,2048]{1,0:T(8,128)(2,1)} %v_ref.5), custom_call_target="tpu_custom_call" | custom-call | tf_op jit(solution)/shard_map/local_state/pallas_call | solution.py:342
  11.8 60.9 %prefix_exchange.1 = (bf16[32,144,128]{2,1,0:T(8,128)(2,1)}, bf16[8,256,256]{2,1,0:T(8,128)(2,1)}) custom-call(bf16[32,144,128]{2,1,0:T(8,128)(2,1)} %local_state.1.refs_0_, bf16[2048,256]{1,0:T(8,128)(2,1)} %refs_1_.1), custom_call_target="tpu_custom_call" | custom-call | tf_op jit(solution)/shard_map/prefix_exchange/pallas_call | solution.py:274
  72.7 23.1 %forward.1 = (bf16[256,4096]{1,0:T(8,128)(2,1)}, f32[256,4096]{1,0:T(8,128)}, bf16[32,144,128]{2,1,0:T(8,128)(2,1)}) custom-call(bf16[256,4096]{1,0:T(8,128)(2,1)} %q_ref.1, bf16[256,4096]{1,0:T(8,128)(2,1)} %k_ref.3, bf16[256,2048]{1,0:T(8,128)(2,1)} %v_ref.5, bf16[8,256,256]{2,1,0:T(8,128)(2,1)} %get-tuple-element.7.t_ref, ...), custom_call_target="tpu_custom_call" | custom-call | tf_op jit(solution)/shard_map/forward/pallas_call | solution.py:352
  95.8 45.1 %suffix_exchange.1.after_ref = bf16[32,144,128]{2,1,0:T(8,128)(2,1)} custom-call(bf16[32,144,128]{2,1,0:T(8,128)(2,1)} %get-tuple-element.11.refs_0_), custom_call_target="tpu_custom_call" | custom-call | tf_op jit(solution)/shard_map/suffix_exchange/pallas_call | solution.py:274
  140.9 11.9 %backward.1 = bf16[256,4096]{1,0:T(8,128)(2,1)} custom-call(bf16[256,2048]{1,0:T(8,128)(2,1)} %v_ref.5, f32[256,4096]{1,0:T(8,128)} %get-tuple-element.10.kl_ref, bf16[32,144,128]{2,1,0:T(8,128)(2,1)} %suffix_exchange.1.after_ref), custom_call_target="tpu_custom_call" | custom-call | tf_op jit(solution)/shard_map/backward/pallas_call | solution.py:366

commit v3 on v1

v3 whole, which is shorter than its diff:
```python
import functools

import jax
import jax.numpy as jnp
from jax import lax
from jax.experimental import pallas as pl
from jax.experimental.pallas import tpu as pltpu
from jax.sharding import PartitionSpec as P

H = 16
SIDE = 16
SPAN = 125.0
F32 = jnp.float32
BF16 = jnp.bfloat16


def dot(a, b, dims):
    return lax.dot_general(a, b, (dims, ((), ())), preferred_element_type=F32)


NN = ((1,), (0,))
NT = ((1,), (1,))
TN = ((0,), (0,))


def split(x):
    hi = x.astype(BF16)
    return hi, (x - hi.astype(F32)).astype(BF16)


def encode(x):
    scale = (jnp.maximum(jnp.max(jnp.abs(x), axis=0, keepdims=True), 1e-20) * 1.01).astype(BF16)
    y = jnp.exp2(jnp.abs(x) * (2 * SPAN / scale.astype(F32)) - SPAN)
    return jnp.where(x < 0, -y, y).astype(BF16), scale


def decode(code, scale):
    y = code.astype(F32)
    x = (jnp.log2(jnp.abs(y)) + SPAN) * (scale.astype(F32) * (0.5 / SPAN))
    return jnp.where(y < 0, -x, x)


def side_rows(scale, row2):
    hi = row2.astype(BF16).astype(F32)
    mid = (row2 - hi).astype(BF16).astype(F32)
    low = row2 - hi - mid
    pad = jnp.zeros((SIDE - 7, row2.shape[1]), F32)
    return jnp.concatenate([scale.astype(F32), hi, mid, low, pad], axis=0).astype(BF16)


def read_side(side):
    s = side.astype(F32)
    return s[0:1], s[1:3] + s[3:5] + s[5:7]


def write_state(ref, piece, state, row):
    width = state.shape[1]
    code, scale = encode(state)
    side = side_rows(scale, jnp.concatenate([row[:, :width], row[:, width:]], axis=0))
    for p in range(state.shape[0] // width):
        ref[piece + p, :width, :] = code[p * width : (p + 1) * width]
        ref[piece + p, width:, :] = side


def read_state(ref, piece, count):
    rows = ref.shape[1] - SIDE
    parts = []
    for p in range(count):
        scale, row2 = read_side(ref[piece + p, rows:, :])
        parts.append(decode(ref[piece + p, :rows, :], scale))
    return jnp.concatenate(parts, axis=0), jnp.concatenate([row2[0:1], row2[1:2]], axis=1)


def remote(src, dst, send, recv, to):
    return pltpu.make_async_remote_copy(
        src_ref=src, dst_ref=dst, send_sem=send, recv_sem=recv, device_id=to,
        device_id_type=pl.DeviceIdType.MESH,
    )


class Exchange:
    def __init__(self, reverse, spans, depth, buffers, kept):
        self.reverse, self.spans, self.depth = reverse, spans, depth
        (self.sent, self.got, self.stage, self.back, self.up_out, self.up_in, self.down_out,
         self.down_in, self.a_send, self.a_recv, self.b_send, self.b_recv, self.u_send,
         self.u_recv, self.d_send, self.d_recv) = buffers
        (self.total, self.above, self.below, self.total_row, self.above_row, self.below_row) = kept
        self.plane = 2 * spans
        self.chunks, self.rows = self.stage.shape[0], self.stage.shape[2] - SIDE
        self.steps = self.chunks + depth - 1
        self.ctx, self.grp = lax.axis_index("ctx"), lax.axis_index("grp")
        self.level = self.grp // 2
        self.mine = self.ctx * 2 + self.grp % 2

    def peer(self, d):
        return (self.mine + d) % self.plane

    def place(self, q):
        return (q // 2, self.level * 2 + q % 2)

    def gather(self, j, d):
        peer = self.peer(d)
        return remote(self.sent.at[peer * self.chunks + j], self.stage.at[j, self.mine],
                      self.a_send.at[j, d - 1], self.a_recv.at[j, d - 1], self.place(peer))

    def scatter(self, j, d):
        peer = self.peer(d)
        return remote(self.back.at[j, peer], self.got.at[self.mine * self.chunks + j],
                      self.b_send.at[j, d - 1], self.b_recv.at[j, d - 1], self.place(peer))

    def upward(self, j):
        return remote(self.up_out.at[j], self.up_in.at[j], self.u_send.at[j], self.u_recv.at[j],
                      (self.ctx, self.grp + 2))

    def downward(self, j):
        return remote(self.down_out.at[j], self.down_in.at[j], self.d_send.at[j],
                      self.d_recv.at[j], (self.ctx, self.grp - 2))

    def load(self, ref, j, k):
        scale, row2 = read_side(ref[j, k, self.rows :, :])
        return decode(ref[j, k, : self.rows, :], scale), row2

    def store(self, ref, j, k, state, row2):
        code, scale = encode(state)
        ref[j, k, : self.rows, :] = code
        ref[j, k, self.rows :, :] = side_rows(scale, row2)

    def chain(self, j, has_in, has_out, copy, in_buf, out_buf, kept, kept_row):
        @pl.when(has_in)
        def _():
            copy(j).wait_recv()
            for k in range(self.spans):
                kept[j, k], kept_row[j, k] = self.load(in_buf, j, k)

        @pl.when(jnp.logical_not(has_in))
        def _():
            for k in range(self.spans):
                kept[j, k] = jnp.zeros_like(kept[j, k])
                kept_row[j, k] = jnp.zeros_like(kept_row[j, k])

        @pl.when(has_out)
        def _():
            for k in range(self.spans):
                self.store(out_buf, j, k, kept[j, k] + self.total[j, k],
                           kept_row[j, k] + self.total_row[j, k])
            copy(j).start()

    def finish(self, j):
        near, near_row = (self.above, self.above_row) if self.reverse else (self.below, self.below_row)
        run = jnp.zeros(self.total.shape[2:], F32)
        run_row = jnp.zeros(self.total_row.shape[2:], F32)
        for i in range(self.spans):
            k = self.spans - 1 - i if self.reverse else i
            one, two = (2 * k + 1, 2 * k) if self.reverse else (2 * k, 2 * k + 1)
            state, row2 = run + near[j, k], run_row + near_row[j, k]
            self.store(self.back, j, one, state, row2)
            beside, beside_row = self.load(self.stage, j, one)
            self.store(self.back, j, two, state + beside, row2 + beside_row)
            run = run + self.below[j, k] + self.total[j, k] + self.above[j, k]
            run_row = run_row + self.below_row[j, k] + self.total_row[j, k] + self.above_row[j, k]
        for d in range(1, self.plane):
            self.scatter(j, d).start()
        self.got[self.mine * self.chunks + j] = self.back[j, self.mine]

    def run(self, beside):
        level, depth, chunks = self.level, self.depth, self.chunks

        def step(t, unused):
            @pl.when(t < chunks)
            def _():
                for d in range(1, self.plane):
                    self.gather(t, d).wait_recv()
                for k in range(self.spans):
                    first, first_row = self.load(self.stage, t, 2 * k)
                    second, second_row = self.load(self.stage, t, 2 * k + 1)
                    self.total[t, k] = first + second
                    self.total_row[t, k] = first_row + second_row

            j_up = t - level

            @pl.when((j_up >= 0) & (j_up < chunks))
            def _():
                self.chain(j_up, level > 0, level < depth - 1, self.upward, self.up_in,
                           self.up_out, self.below, self.below_row)

            j_down = t - (depth - 1 - level)

            @pl.when((j_down >= 0) & (j_down < chunks))
            def _():
                self.chain(j_down, level < depth - 1, level > 0, self.downward, self.down_in,
                           self.down_out, self.above, self.above_row)

            j_end = t - (depth - 1)

            @pl.when(j_end >= 0)
            def _():
                self.finish(j_end)

            beside(t + 1)
            return unused

        beside(0)
        lax.fori_loop(0, self.steps, step, 0)

    def each_head(self, work):
        per_head = 2
        for jj in range(self.chunks // per_head):

            def one(i, unused, jj=jj):
                peer = self.peer(i + 1)
                work(peer * (self.chunks // per_head) + jj, per_head * jj, i + 1)
                return unused

            lax.fori_loop(0, self.plane, one, 0)

    def send(self, chunk, d):
        @pl.when(d < self.plane)
        def _():
            self.gather(chunk, d).start()
            self.gather(chunk + 1, d).start()

        @pl.when(d == self.plane)
        def _():
            for j in (chunk, chunk + 1):
                self.stage[j, self.mine] = self.sent[self.mine * self.chunks + j]

    def receive(self, chunk, d):
        @pl.when(d < self.plane)
        def _():
            self.scatter(chunk, self.plane - d).wait_recv()
            self.scatter(chunk + 1, self.plane - d).wait_recv()

    def drain(self):
        for j in range(self.chunks):
            for d in range(1, self.plane):
                self.gather(j, d).wait_send()
                self.scatter(j, d).wait_send()

        @pl.when(self.level < self.depth - 1)
        def _():
            for j in range(self.chunks):
                self.upward(j).wait_send()

        @pl.when(self.level > 0)
        def _():
            for j in range(self.chunks):
                self.downward(j).wait_send()


def kernel(spans, depth, scale, q_ref, k_ref, v_ref, teacher_ref, qg_ref, kg_ref, *scratch):
    kept, first, second = scratch[:6], scratch[6:22], scratch[22:38]
    (target, numer_ref, denom_ref, hi_ref, lo_ref, dd_ref, kl_ref, t_send, t_recv, t_own) = scratch[38:]
    prefix = Exchange(False, spans, depth, first, kept)
    suffix = Exchange(True, spans, depth, second, kept)
    ctx, grp, plane, groups = prefix.ctx, prefix.grp, 2 * spans, 2 * depth
    rows = q_ref.shape[0]
    feat, width = q_ref.shape[1] // H, v_ref.shape[1] // H
    per_head = feat // width
    per_group = H // groups
    causal = lax.broadcasted_iota(jnp.int32, (rows, rows), 1) <= lax.broadcasted_iota(
        jnp.int32, (rows, rows), 0
    )

    def cols(head, w):
        return pl.ds(pl.multiple_of(head * w, w), w)

    def greet(to):
        pl.semaphore_signal(barrier, inc=1, device_id=to, device_id_type=pl.DeviceIdType.MESH)

    barrier = pltpu.get_barrier_semaphore()
    for d in range(1, plane):
        greet(prefix.place(prefix.peer(d)))
    for d in range(1, groups):
        greet((ctx, (grp + d) % groups))
    pl.semaphore_wait(barrier, plane + groups - 2)

    def give(d):
        peer = (grp + d) % groups
        return remote(teacher_ref.at[pl.ds(peer * rows, rows)], target.at[grp], t_send.at[d - 1],
                      t_recv.at[d - 1], (ctx, peer))

    own = pltpu.make_async_copy(teacher_ref.at[pl.ds(grp * rows, rows)], target.at[grp], t_own)
    own.start()

    def local(head, chunk, d):
        k = k_ref[:, cols(head, feat)]
        state = dot(k, v_ref[:, cols(head, width)], TN)
        write_state(prefix.sent, head * per_head, state, jnp.sum(k.astype(F32), axis=0, keepdims=True))
        prefix.send(chunk, d)

    prefix.each_head(local)

    def scores_of(head):
        q, k, v = q_ref[:, cols(head, feat)], k_ref[:, cols(head, feat)], v_ref[:, cols(head, width)]
        scores = jnp.where(causal, dot(q, k, NT), 0.0)
        s_hi, s_lo = split(scores)
        numer_ref[head] = dot(s_hi, v, NN) + dot(s_lo, v, NN)
        denom_ref[head] = jnp.sum(scores, axis=1, keepdims=True)

    def beside_prefix(t):
        for i in (1, 2):
            @pl.when(2 * t + i < groups)
            def _():
                give(2 * t + i).start()

        @pl.when(t < H // 2)
        def _():
            scores_of(2 * t)
            scores_of(2 * t + 1)

    prefix.run(beside_prefix)
    for t in range(prefix.steps + 1, max(H // 2, groups // 2)):
        beside_prefix(t)
    for d in range(1, groups):
        give(d).wait()
    own.wait()

    def forward(head, chunk, d):
        prefix.receive(chunk, d)
        q = q_ref[:, cols(head, feat)]
        q_wide = q.astype(F32)
        kv, key_row = read_state(prefix.got, head * per_head, per_head)
        kv_hi, kv_lo = split(kv)
        numer = numer_ref[head] + dot(q, kv_hi, NN) + dot(q, kv_lo, NN)
        denom = denom_ref[head] + jnp.sum(q_wide * key_row, axis=1, keepdims=True)
        inv = 1.0 / denom
        student = numer * inv
        resid = student - target[head // per_group, :, cols(head % per_group, width)].astype(F32)
        d_denom = -jnp.sum(resid * student, axis=1, keepdims=True) * inv
        dn_hi, dn_lo = split(resid * inv)
        hi_ref[head] = dn_hi
        lo_ref[head] = dn_lo
        dd_ref[head] = d_denom
        adj = dot(q, dn_hi, TN) + dot(q, dn_lo, TN)
        write_state(suffix.sent, head * per_head, adj, jnp.sum(d_denom * q_wide, axis=0, keepdims=True))
        suffix.send(chunk, d)

    prefix.each_head(forward)

    def grads_of(head):
        q, k, v = q_ref[:, cols(head, feat)], k_ref[:, cols(head, feat)], v_ref[:, cols(head, width)]
        dn_hi, dn_lo, d_denom = hi_ref[head], lo_ref[head], dd_ref[head]
        kv, key_row = read_state(prefix.got, head * per_head, per_head)
        kv_hi, kv_lo = split(kv)
        mixed = jnp.where(causal, dot(dn_hi, v, NT) + dot(dn_lo, v, NT) + d_denom, 0.0)
        m_hi, m_lo = split(mixed)
        q_grad = dot(m_hi, k, NN) + dot(m_lo, k, NN)
        q_grad = q_grad + dot(dn_hi, kv_hi, NT) + dot(dn_hi, kv_lo, NT) + dot(dn_lo, kv_hi, NT)
        q_grad = q_grad + d_denom * key_row
        qg_ref[:, cols(head, feat)] = (scale * q_grad).astype(BF16)
        kl_ref[head] = dot(m_hi, q, TN) + dot(m_lo, q, TN)

    def beside_suffix(t):
        @pl.when(t < H // 2)
        def _():
            grads_of(2 * t)
            grads_of(2 * t + 1)

    suffix.run(beside_suffix)
    for t in range(suffix.steps + 1, H // 2):
        beside_suffix(t)

    def backward(head, chunk, d):
        suffix.receive(chunk, d)
        adj, row = read_state(suffix.got, head * per_head, per_head)
        a_hi, a_lo = split(adj)
        v = v_ref[:, cols(head, width)]
        k_grad = kl_ref[head] + dot(v, a_hi, NT) + dot(v, a_lo, NT) + row
        kg_ref[:, cols(head, feat)] = (scale * k_grad).astype(BF16)

    suffix.each_head(backward)
    prefix.drain()
    suffix.drain()


def on_device(spans, groups, query_feat, key_feat, values, teacher):
    rows = query_feat.shape[0]
    feat = query_feat.shape[1] // H
    width = values.shape[1] // H
    scale = float(rows * spans * groups) ** 0.5
    depth, plane = groups // 2, 2 * spans
    pieces = H * feat // width
    chunks = pieces // plane
    length = width + SIDE
    dma = pltpu.SemaphoreType.DMA
    vmem = pl.BlockSpec(memory_space=pltpu.VMEM)
    whole = pltpu.VMEM((pieces, length, width), BF16)
    block = pltpu.VMEM((chunks, plane, length, width), BF16)
    line = pltpu.VMEM((chunks, spans, length, width), BF16)
    wide = pltpu.VMEM((chunks, spans, width, width), F32)
    row = pltpu.VMEM((chunks, spans, 2, width), F32)
    phase = [whole] * 2 + [block] * 2 + [line] * 4 + [dma((chunks, plane - 1))] * 4 + [dma((chunks,))] * 4
    column = pltpu.VMEM((H, rows, 1), F32)
    half = pltpu.VMEM((H, rows, width), BF16)
    scratch = [wide] * 3 + [row] * 3 + phase + phase + [
        pltpu.VMEM((groups, rows, teacher.shape[1]), BF16),
        pltpu.VMEM((H, rows, width), F32),
        column, half, half, column,
        pltpu.VMEM((H, rows, feat), F32),
        dma((groups - 1,)), dma((groups - 1,)), dma,
    ]
    out = jax.ShapeDtypeStruct((rows, H * feat), BF16)
    return pl.pallas_call(
        functools.partial(kernel, spans, depth, scale),
        in_specs=[vmem, vmem, vmem, pl.BlockSpec(memory_space=pl.ANY)],
        out_specs=[vmem, vmem],
        out_shape=[out, out],
        scratch_shapes=scratch,
        compiler_params=pltpu.CompilerParams(
            collective_id=0, has_side_effects=True, vmem_limit_bytes=60 * 1024 * 1024
        ),
        name="grads",
    )(query_feat, key_feat, values, teacher)


def solution(mesh):
    placed = (
        P(("ctx", "grp"), None),
        P(("ctx", "grp"), None),
        P(("ctx", "grp"), None),
        P("ctx", "grp"),
    )
    return jax.shard_map(
        functools.partial(on_device, mesh.shape["ctx"], mesh.shape["grp"]),
        mesh=mesh,
        in_specs=placed,
        out_specs=(P(("ctx", "grp"), None), P(("ctx", "grp"), None)),
        check_vma=False,
    )
```

time: 212 us -> 118 us (0.56)
  blocking collectives: 102 us -> 0 us
  Pallas kernels: 39.7 us -> 113 us
  waiting for transfers between devices: 51.5 us -> 0 us
  starting transfers between devices: 7.75 us -> 0 us
  local copies, waits for them, and re-layouts: 9.06 us -> 4.6 us
    all_to_all x3 -> x0, blocking collectives: 102 us -> none  [swap(): return lax.all_to_all(x, everyone, split_axis=0, concat_axis=0, tiled=True)]
    pallas_call x5 -> x1, Pallas kernels: 39.7 us -> 113 us  [on_device(): pl.pallas_call(functools.partial(kernel, spans, depth, scale), in_specs=[...]
    all_to_all x2 -> x0, waiting for transfers between devices: 51.5 us -> none  [the longest x1 28 us: swap(): return lax.all_to_all(x, everyone, split_axis=0, concat_axis=0, tiled=True)]
    all_to_all x2 -> x0, starting transfers between devices: 7.75 us -> none  [the longest x1 4.25 us: on_device(): lax.all_to_all(teacher, 'grp', split_axis=0, concat_axis=1, tiled=True)]
    all_to_all x1 -> x0, local copies, waits for them, and re-layouts: 2.41 us -> none  [on_device(): lax.all_to_all(teacher, 'grp', split_axis=0, concat_axis=1, tiled=True)]
    unnamed x14 -> x4, local copies, waits for them, and re-layouts: 6.64 us -> 4.6 us
  transfers between devices with their start and end apart: 2 -> 0, of which waited for: 2 -> 0; matrix products, arithmetic and copies ran while one was open for 1% -> 0% of each run, Pallas kernels for 1% -> 0%
where the time goes in v3:
time: 118 us
  Pallas kernels  113 us (96%)
  local copies, waits for them, and re-layouts  4.6 us (4%)
    pallas_call x1, Pallas kernels, on_device(): pl.pallas_call(functools.partial(kernel, spans, depth, scale), in_specs=[...  113 us
    unnamed x4, local copies, waits for them, and re-layouts  4.6 us

profile of v3, /device:TPU:0, one launch (start us, length us, event | category | flops | bytes accessed | tf_op | source)
XLA Modules:
  0.0 118.0 jit_solution(7136285928202322386)
XLA Ops:
  0.6 112.8 %grads.1 = (bf16[256,4096]{1,0:T(8,128)(2,1)}, bf16[256,4096]{1,0:T(8,128)(2,1)}) custom-call(bf16[256,4096]{1,0:T(8,128)(2,1)} %q_ref.1, bf16[256,4096]{1,0:T(8,128)(2,1)} %k_ref.1, bf16[256,2048]{1,0:T(8,128)(2,1)} %v_ref.1, bf16[2048,256]{1,0:T(8,128)(2,1)} %teacher_ref.1), custom_call_target="tpu_custom_call" | custom-call | tf_op jit(solution)/shard_map/grads/pallas_call | solution.py:403
  113.4 0.0 copy-start
  113.4 3.3 %copy.8 = bf16[256,4096]{1,0:T(8,128)(2,1)} copy(bf16[256,4096]{1,0:T(8,128)(2,1)} %get-tuple-element.4) | data formatting | bytes 4194304
  116.7 0.0 copy-done
  116.7 1.3 %copy.9 = bf16[256,4096]{1,0:T(8,128)(2,1)} copy(bf16[256,4096]{1,0:T(8,128)(2,1)S(1)} %copy-done) | data formatting | bytes 4194304
Async XLA Ops:
  113.4 3.3 %copy-start = (bf16[256,4096]{1,0:T(8,128)(2,1)S(1)}, bf16[256,4096]{1,0:T(8,128)(2,1)}, u32[]{:S(2)}) copy-start(bf16[256,4096]{1,0:T(8,128)(2,1)} %get-tuple-element.5) | copy-start | bytes 6291460

commit v4 on v3

--- a/solution.py
+++ b/solution.py
@@ -162,56 +162,45 @@
             self.scatter(j, d).start()
         self.got[self.mine * self.chunks + j] = self.back[j, self.mine]
 
-    def run(self, beside):
+    def step(self, t):
         level, depth, chunks = self.level, self.depth, self.chunks
 
-        def step(t, unused):
-            @pl.when(t < chunks)
-            def _():
-                for d in range(1, self.plane):
-                    self.gather(t, d).wait_recv()
-                for k in range(self.spans):
-                    first, first_row = self.load(self.stage, t, 2 * k)
-                    second, second_row = self.load(self.stage, t, 2 * k + 1)
-                    self.total[t, k] = first + second
-                    self.total_row[t, k] = first_row + second_row
-
-            j_up = t - level
-
-            @pl.when((j_up >= 0) & (j_up < chunks))
-            def _():
-                self.chain(j_up, level > 0, level < depth - 1, self.upward, self.up_in,
-                           self.up_out, self.below, self.below_row)
-
-            j_down = t - (depth - 1 - level)
-
-            @pl.when((j_down >= 0) & (j_down < chunks))
-            def _():
-                self.chain(j_down, level < depth - 1, level > 0, self.downward, self.down_in,
-                           self.down_out, self.above, self.above_row)
-
-            j_end = t - (depth - 1)
-
-            @pl.when(j_end >= 0)
-            def _():
-                self.finish(j_end)
-
-            beside(t + 1)
+        @pl.when((t >= 0) & (t < chunks))
+        def _():
+            for d in range(1, self.plane):
+                self.gather(t, d).wait_recv()
+            for k in range(self.spans):
+                first, first_row = self.load(self.stage, t, 2 * k)
+                second, second_row = self.load(self.stage, t, 2 * k + 1)
+                self.total[t, k] = first + second
+                self.total_row[t, k] = first_row + second_row
+
+        j_up = t - level
+
+        @pl.when((j_up >= 0) & (j_up < chunks))
+        def _():
+            self.chain(j_up, level > 0, level < depth - 1, self.upward, self.up_in,
+                       self.up_out, self.below, self.below_row)
+
+        j_down = t - (depth - 1 - level)
+
+        @pl.when((j_down >= 0) & (j_down < chunks))
+        def _():
+            self.chain(j_down, level < depth - 1, level > 0, self.downward, self.down_in,
+                       self.down_out, self.above, self.above_row)
+
+        j_end = t - (depth - 1)
+
+        @pl.when((j_end >= 0) & (j_end < chunks))
+        def _():
+            self.finish(j_end)
+
+    def each_head(self, group, work):
+        def one(i, unused):
+            work(self.peer(i + 1) * (self.chunks // 2) + group, 2 * group, i + 1)
             return unused
 
-        beside(0)
-        lax.fori_loop(0, self.steps, step, 0)
-
-    def each_head(self, work):
-        per_head = 2
-        for jj in range(self.chunks // per_head):
-
-            def one(i, unused, jj=jj):
-                peer = self.peer(i + 1)
-                work(peer * (self.chunks // per_head) + jj, per_head * jj, i + 1)
-                return unused
-
-            lax.fori_loop(0, self.plane, one, 0)
+        lax.fori_loop(0, self.plane, one, 0)
 
     def send(self, chunk, d):
         @pl.when(d < self.plane)
@@ -248,15 +237,16 @@
 
 
 def kernel(spans, depth, scale, q_ref, k_ref, v_ref, teacher_ref, qg_ref, kg_ref, *scratch):
-    kept, first, second = scratch[:6], scratch[6:22], scratch[22:38]
-    (target, numer_ref, denom_ref, hi_ref, lo_ref, dd_ref, kl_ref, t_send, t_recv, t_own) = scratch[38:]
-    prefix = Exchange(False, spans, depth, first, kept)
-    suffix = Exchange(True, spans, depth, second, kept)
+    first, second = scratch[:22], scratch[22:44]
+    (target, numer_ref, denom_ref, hi_ref, lo_ref, dd_ref, kl_ref, t_send, t_recv, t_own) = scratch[44:]
+    prefix = Exchange(False, spans, depth, first[6:], first[:6])
+    suffix = Exchange(True, spans, depth, second[6:], second[:6])
     ctx, grp, plane, groups = prefix.ctx, prefix.grp, 2 * spans, 2 * depth
     rows = q_ref.shape[0]
     feat, width = q_ref.shape[1] // H, v_ref.shape[1] // H
     per_head = feat // width
     per_group = H // groups
+    heads_each = H // plane
     causal = lax.broadcasted_iota(jnp.int32, (rows, rows), 1) <= lax.broadcasted_iota(
         jnp.int32, (rows, rows), 0
     )
@@ -281,6 +271,8 @@
 
     own = pltpu.make_async_copy(teacher_ref.at[pl.ds(grp * rows, rows)], target.at[grp], t_own)
     own.start()
+    for d in range(2, groups, 2):
+        give(d).start()
 
     def local(head, chunk, d):
         k = k_ref[:, cols(head, feat)]
@@ -288,7 +280,8 @@
         write_state(prefix.sent, head * per_head, state, jnp.sum(k.astype(F32), axis=0, keepdims=True))
         prefix.send(chunk, d)
 
-    prefix.each_head(local)
+    for group in range(heads_each):
+        prefix.each_head(group, local)
 
     def scores_of(head):
         q, k, v = q_ref[:, cols(head, feat)], k_ref[:, cols(head, feat)], v_ref[:, cols(head, width)]
@@ -296,24 +289,6 @@
         s_hi, s_lo = split(scores)
         numer_ref[head] = dot(s_hi, v, NN) + dot(s_lo, v, NN)
         denom_ref[head] = jnp.sum(scores, axis=1, keepdims=True)
-
-    def beside_prefix(t):
-        for i in (1, 2):
-            @pl.when(2 * t + i < groups)
-            def _():
-                give(2 * t + i).start()
-
-        @pl.when(t < H // 2)
-        def _():
-            scores_of(2 * t)
-            scores_of(2 * t + 1)
-
-    prefix.run(beside_prefix)
-    for t in range(prefix.steps + 1, max(H // 2, groups // 2)):
-        beside_prefix(t)
-    for d in range(1, groups):
-        give(d).wait()
-    own.wait()
 
     def forward(head, chunk, d):
         prefix.receive(chunk, d)
@@ -335,8 +310,6 @@
         write_state(suffix.sent, head * per_head, adj, jnp.sum(d_denom * q_wide, axis=0, keepdims=True))
         suffix.send(chunk, d)
 
-    prefix.each_head(forward)
-
     def grads_of(head):
         q, k, v = q_ref[:, cols(head, feat)], k_ref[:, cols(head, feat)], v_ref[:, cols(head, width)]
         dn_hi, dn_lo, d_denom = hi_ref[head], lo_ref[head], dd_ref[head]
@@ -350,15 +323,49 @@
         qg_ref[:, cols(head, feat)] = (scale * q_grad).astype(BF16)
         kl_ref[head] = dot(m_hi, q, TN) + dot(m_lo, q, TN)
 
-    def beside_suffix(t):
-        @pl.when(t < H // 2)
-        def _():
-            grads_of(2 * t)
-            grads_of(2 * t + 1)
-
-    suffix.run(beside_suffix)
-    for t in range(suffix.steps + 1, H // 2):
-        beside_suffix(t)
+    def grads_at(i):
+        grads_of(i % plane * heads_each + i // plane)
+
+    steps, begin = prefix.steps, depth + 2
+    quick, slow = 4, min(2, H // steps)
+
+    def scores_at(t):
+        @pl.when(t < H // quick)
+        def _():
+            for i in range(quick):
+                scores_of(quick * t + i)
+
+    def step(t, unused):
+        prefix.step(t)
+
+        @pl.when(2 * t + 1 < groups)
+        def _():
+            give(2 * t + 1).start()
+
+        scores_at(t + 1)
+        for group in range(heads_each):
+
+            @pl.when(t == depth + 1 + 2 * group)
+            def _():
+                if group == 0:
+                    for d in range(1, groups):
+                        give(d).wait()
+                    own.wait()
+                prefix.each_head(group, forward)
+
+        suffix.step(t - begin)
+
+        @pl.when(t >= begin)
+        def _():
+            for i in range(slow):
+                grads_at(slow * (t - begin) + i)
+
+        return unused
+
+    scores_at(0)
+    lax.fori_loop(0, begin + steps, step, 0)
+    for i in range(slow * steps, H):
+        grads_at(i)
 
     def backward(head, chunk, d):
         suffix.receive(chunk, d)
@@ -368,7 +375,8 @@
         k_grad = kl_ref[head] + dot(v, a_hi, NT) + dot(v, a_lo, NT) + row
         kg_ref[:, cols(head, feat)] = (scale * k_grad).astype(BF16)
 
-    suffix.each_head(backward)
+    for group in range(heads_each):
+        suffix.each_head(group, backward)
     prefix.drain()
     suffix.drain()
 
@@ -389,10 +397,10 @@
     line = pltpu.VMEM((chunks, spans, length, width), BF16)
     wide = pltpu.VMEM((chunks, spans, width, width), F32)
     row = pltpu.VMEM((chunks, spans, 2, width), F32)
-    phase = [whole] * 2 + [block] * 2 + [line] * 4 + [dma((chunks, plane - 1))] * 4 + [dma((chunks,))] * 4
+    phase = [wide] * 3 + [row] * 3 + [whole] * 2 + [block] * 2 + [line] * 4 + [dma((chunks, plane - 1))] * 4 + [dma((chunks,))] * 4
     column = pltpu.VMEM((H, rows, 1), F32)
     half = pltpu.VMEM((H, rows, width), BF16)
-    scratch = [wide] * 3 + [row] * 3 + phase + phase + [
+    scratch = phase + phase + [
         pltpu.VMEM((groups, rows, teacher.shape[1]), BF16),
         pltpu.VMEM((H, rows, width), F32),
         column, half, half, column,

time: 118 us -> 112 us (0.949)
  Pallas kernels: 113 us -> 106 us
    pallas_call x1, Pallas kernels: 113 us -> 106 us  [on_device(): pl.pallas_call(functools.partial(kernel, spans, depth, scale), in_specs=[...]
where the time goes in v4:
time: 112 us
  Pallas kernels  106 us (95%)
  local copies, waits for them, and re-layouts  4.6 us (4%)
    pallas_call x1, Pallas kernels, on_device(): pl.pallas_call(functools.partial(kernel, spans, depth, scale), in_specs=[...  106 us
    unnamed x4, local copies, waits for them, and re-layouts  4.6 us

profile of v4, /device:TPU:0, one launch (start us, length us, event | category | flops | bytes accessed | tf_op | source)
XLA Modules:
  0.0 111.5 jit_solution(2567914337530040992)
XLA Ops:
  0.6 106.3 %grads.1 = (bf16[256,4096]{1,0:T(8,128)(2,1)}, bf16[256,4096]{1,0:T(8,128)(2,1)}) custom-call(bf16[256,4096]{1,0:T(8,128)(2,1)} %q_ref.1, bf16[256,4096]{1,0:T(8,128)(2,1)} %k_ref.1, bf16[256,2048]{1,0:T(8,128)(2,1)} %v_ref.1, bf16[2048,256]{1,0:T(8,128)(2,1)} %teacher_ref.1), custom_call_target="tpu_custom_call" | custom-call | tf_op jit(solution)/shard_map/grads/pallas_call | solution.py:411
  106.9 0.0 copy-start
  106.9 3.3 %copy.8 = bf16[256,4096]{1,0:T(8,128)(2,1)} copy(bf16[256,4096]{1,0:T(8,128)(2,1)} %get-tuple-element.4) | data formatting | bytes 4194304
  110.2 0.0 copy-done
  110.2 1.3 %copy.9 = bf16[256,4096]{1,0:T(8,128)(2,1)} copy(bf16[256,4096]{1,0:T(8,128)(2,1)S(1)} %copy-done) | data formatting | bytes 4194304
Async XLA Ops:
  106.9 3.3 %copy-start = (bf16[256,4096]{1,0:T(8,128)(2,1)S(1)}, bf16[256,4096]{1,0:T(8,128)(2,1)}, u32[]{:S(2)}) copy-start(bf16[256,4096]{1,0:T(8,128)(2,1)} %get-tuple-element.5) | copy-start | bytes 6291460

commit v5 on v4

--- a/solution.py
+++ b/solution.py
@@ -86,27 +86,34 @@
          self.u_recv, self.d_send, self.d_recv) = buffers
         (self.total, self.above, self.below, self.total_row, self.above_row, self.below_row) = kept
         self.plane = 2 * spans
-        self.chunks, self.rows = self.stage.shape[0], self.stage.shape[2] - SIDE
+        self.chunks, self.rows = self.back.shape[0], self.back.shape[2] - SIDE
         self.steps = self.chunks + depth - 1
         self.ctx, self.grp = lax.axis_index("ctx"), lax.axis_index("grp")
-        self.level = self.grp // 2
-        self.mine = self.ctx * 2 + self.grp % 2
+        self.level = lax.div(self.grp, 2)
+        self.mine = self.ctx * 2 + lax.rem(self.grp, 2)
+        self.peers = [self.peer(d) for d in range(self.plane)]
+        self.places = [self.place(q) for q in self.peers]
 
     def peer(self, d):
-        return (self.mine + d) % self.plane
+        return lax.rem(self.mine + d, self.plane)
 
     def place(self, q):
-        return (q // 2, self.level * 2 + q % 2)
-
-    def gather(self, j, d):
-        peer = self.peer(d)
-        return remote(self.sent.at[peer * self.chunks + j], self.stage.at[j, self.mine],
-                      self.a_send.at[j, d - 1], self.a_recv.at[j, d - 1], self.place(peer))
+        return (lax.div(q, 2), self.level * 2 + lax.rem(q, 2))
+
+    def at(self, d):
+        if isinstance(d, int):
+            return self.peers[d], self.places[d]
+        return self.peer(d), self.place(self.peer(d))
+
+    def gather(self, g, d):
+        peer, place = self.at(d)
+        return remote(self.sent.at[pl.ds(peer * self.chunks + 2 * g, 2)], self.stage.at[g, self.mine],
+                      self.a_send.at[g, d - 1], self.a_recv.at[g, d - 1], place)
 
     def scatter(self, j, d):
-        peer = self.peer(d)
+        peer, place = self.at(d)
         return remote(self.back.at[j, peer], self.got.at[self.mine * self.chunks + j],
-                      self.b_send.at[j, d - 1], self.b_recv.at[j, d - 1], self.place(peer))
+                      self.b_send.at[j, d - 1], self.b_recv.at[j, d - 1], place)
 
     def upward(self, j):
         return remote(self.up_out.at[j], self.up_in.at[j], self.u_send.at[j], self.u_recv.at[j],
@@ -119,6 +126,11 @@
     def load(self, ref, j, k):
         scale, row2 = read_side(ref[j, k, self.rows :, :])
         return decode(ref[j, k, : self.rows, :], scale), row2
+
+    def staged(self, j, k):
+        half, side = lax.div(j, 2), lax.rem(j, 2)
+        scale, row2 = read_side(self.stage[half, k, side, self.rows :, :])
+        return decode(self.stage[half, k, side, : self.rows, :], scale), row2
 
     def store(self, ref, j, k, state, row2):
         code, scale = encode(state)
@@ -154,7 +166,7 @@
             one, two = (2 * k + 1, 2 * k) if self.reverse else (2 * k, 2 * k + 1)
             state, row2 = run + near[j, k], run_row + near_row[j, k]
             self.store(self.back, j, one, state, row2)
-            beside, beside_row = self.load(self.stage, j, one)
+            beside, beside_row = self.staged(j, one)
             self.store(self.back, j, two, state + beside, row2 + beside_row)
             run = run + self.below[j, k] + self.total[j, k] + self.above[j, k]
             run_row = run_row + self.below_row[j, k] + self.total_row[j, k] + self.above_row[j, k]
@@ -165,13 +177,16 @@
     def step(self, t):
         level, depth, chunks = self.level, self.depth, self.chunks
 
+        @pl.when((t >= 0) & (t < chunks) & (lax.rem(t, 2) == 0))
+        def _():
+            for d in range(1, self.plane):
+                self.gather(lax.div(t, 2), d).wait_recv()
+
         @pl.when((t >= 0) & (t < chunks))
         def _():
-            for d in range(1, self.plane):
-                self.gather(t, d).wait_recv()
             for k in range(self.spans):
-                first, first_row = self.load(self.stage, t, 2 * k)
-                second, second_row = self.load(self.stage, t, 2 * k + 1)
+                first, first_row = self.staged(t, 2 * k)
+                second, second_row = self.staged(t, 2 * k + 1)
                 self.total[t, k] = first + second
                 self.total_row[t, k] = first_row + second_row
 
@@ -205,13 +220,12 @@
     def send(self, chunk, d):
         @pl.when(d < self.plane)
         def _():
-            self.gather(chunk, d).start()
-            self.gather(chunk + 1, d).start()
+            self.gather(chunk // 2, d).start()
 
         @pl.when(d == self.plane)
         def _():
-            for j in (chunk, chunk + 1):
-                self.stage[j, self.mine] = self.sent[self.mine * self.chunks + j]
+            for i in range(2):
+                self.stage[chunk // 2, self.mine, i] = self.sent[self.mine * self.chunks + chunk + i]
 
     def receive(self, chunk, d):
         @pl.when(d < self.plane)
@@ -222,8 +236,10 @@
     def drain(self):
         for j in range(self.chunks):
             for d in range(1, self.plane):
-                self.gather(j, d).wait_send()
                 self.scatter(j, d).wait_send()
+        for g in range(self.chunks // 2):
+            for d in range(1, self.plane):
+                self.gather(g, d).wait_send()
 
         @pl.when(self.level < self.depth - 1)
         def _():
@@ -236,7 +252,13 @@
                 self.downward(j).wait_send()
 
 
-def kernel(spans, depth, scale, q_ref, k_ref, v_ref, teacher_ref, qg_ref, kg_ref, *scratch):
+def kernel(spans, depth, scale, q_hbm, k_hbm, v_hbm, teacher_ref, qg_ref, kg_ref, q_ref, k_ref, v_ref, in_sem, *scratch):
+    loads = [
+        pltpu.make_async_copy(src, dst, in_sem.at[i])
+        for i, (src, dst) in enumerate(((k_hbm, k_ref), (v_hbm, v_ref), (q_hbm, q_ref)))
+    ]
+    for load in loads:
+        load.start()
     first, second = scratch[:22], scratch[22:44]
     (target, numer_ref, denom_ref, hi_ref, lo_ref, dd_ref, kl_ref, t_send, t_recv, t_own) = scratch[44:]
     prefix = Exchange(False, spans, depth, first[6:], first[:6])
@@ -259,13 +281,13 @@
 
     barrier = pltpu.get_barrier_semaphore()
     for d in range(1, plane):
-        greet(prefix.place(prefix.peer(d)))
+        greet(prefix.places[d])
     for d in range(1, groups):
-        greet((ctx, (grp + d) % groups))
+        greet((ctx, lax.rem(grp + d, groups)))
     pl.semaphore_wait(barrier, plane + groups - 2)
 
     def give(d):
-        peer = (grp + d) % groups
+        peer = lax.rem(grp + d, groups)
         return remote(teacher_ref.at[pl.ds(peer * rows, rows)], target.at[grp], t_send.at[d - 1],
                       t_recv.at[d - 1], (ctx, peer))
 
@@ -273,6 +295,9 @@
     own.start()
     for d in range(2, groups, 2):
         give(d).start()
+
+    loads[0].wait()
+    loads[1].wait()
 
     def local(head, chunk, d):
         k = k_ref[:, cols(head, feat)]
@@ -300,7 +325,7 @@
         denom = denom_ref[head] + jnp.sum(q_wide * key_row, axis=1, keepdims=True)
         inv = 1.0 / denom
         student = numer * inv
-        resid = student - target[head // per_group, :, cols(head % per_group, width)].astype(F32)
+        resid = student - target[lax.div(head, per_group), :, cols(lax.rem(head, per_group), width)].astype(F32)
         d_denom = -jnp.sum(resid * student, axis=1, keepdims=True) * inv
         dn_hi, dn_lo = split(resid * inv)
         hi_ref[head] = dn_hi
@@ -324,7 +349,7 @@
         kl_ref[head] = dot(m_hi, q, TN) + dot(m_lo, q, TN)
 
     def grads_at(i):
-        grads_of(i % plane * heads_each + i // plane)
+        grads_of(lax.rem(i, plane) * heads_each + lax.div(i, plane))
 
     steps, begin = prefix.steps, depth + 2
     quick, slow = 4, min(2, H // steps)
@@ -362,10 +387,11 @@
 
         return unused
 
+    loads[2].wait()
     scores_at(0)
     lax.fori_loop(0, begin + steps, step, 0)
     for i in range(slow * steps, H):
-        grads_at(i)
+        grads_of(i % plane * heads_each + i // plane)
 
     def backward(head, chunk, d):
         suffix.receive(chunk, d)
@@ -379,6 +405,11 @@
         suffix.each_head(group, backward)
     prefix.drain()
     suffix.drain()
+
+
+def deliver_kernel(q_in, k_in, q_out, k_out):
+    q_out[...] = q_in[...]
+    k_out[...] = k_in[...]
 
 
 def on_device(spans, groups, query_feat, key_feat, values, teacher):
@@ -397,10 +428,13 @@
     line = pltpu.VMEM((chunks, spans, length, width), BF16)
     wide = pltpu.VMEM((chunks, spans, width, width), F32)
     row = pltpu.VMEM((chunks, spans, 2, width), F32)
-    phase = [wide] * 3 + [row] * 3 + [whole] * 2 + [block] * 2 + [line] * 4 + [dma((chunks, plane - 1))] * 4 + [dma((chunks,))] * 4
+    pairs = pltpu.VMEM((chunks // 2, plane, 2, length, width), BF16)
+    phase = [wide] * 3 + [row] * 3 + [whole] * 2 + [pairs, block] + [line] * 4
+    phase += [dma((chunks // 2, plane - 1))] * 2 + [dma((chunks, plane - 1))] * 2 + [dma((chunks,))] * 4
     column = pltpu.VMEM((H, rows, 1), F32)
     half = pltpu.VMEM((H, rows, width), BF16)
-    scratch = phase + phase + [
+    scratch = [pltpu.VMEM(x.shape, BF16) for x in (query_feat, key_feat, values)] + [dma((3,))]
+    scratch += phase + phase + [
         pltpu.VMEM((groups, rows, teacher.shape[1]), BF16),
         pltpu.VMEM((H, rows, width), F32),
         column, half, half, column,
@@ -408,9 +442,9 @@
         dma((groups - 1,)), dma((groups - 1,)), dma,
     ]
     out = jax.ShapeDtypeStruct((rows, H * feat), BF16)
-    return pl.pallas_call(
+    grads = pl.pallas_call(
         functools.partial(kernel, spans, depth, scale),
-        in_specs=[vmem, vmem, vmem, pl.BlockSpec(memory_space=pl.ANY)],
+        in_specs=[pl.BlockSpec(memory_space=pl.ANY)] * 4,
         out_specs=[vmem, vmem],
         out_shape=[out, out],
         scratch_shapes=scratch,
@@ -419,6 +453,16 @@
         ),
         name="grads",
     )(query_feat, key_feat, values, teacher)
+    slab = pl.BlockSpec((rows // 4, H * feat), lambda i: (i, 0))
+    return pl.pallas_call(
+        deliver_kernel,
+        grid=(4,),
+        in_specs=[slab, slab],
+        out_specs=[slab, slab],
+        out_shape=[out, out],
+        compiler_params=pltpu.CompilerParams(vmem_limit_bytes=60 * 1024 * 1024),
+        name="deliver",
+    )(*grads)
 
 
 def solution(mesh):

time: 112 us -> 111 us (level)
  Pallas kernels: 106 us -> 111 us
  local copies, waits for them, and re-layouts: 4.6 us -> 0 us
    pallas_call x0 -> x1, Pallas kernels: none -> 4.68 us  [on_device(): pl.pallas_call(deliver_kernel, grid=(4,), in_specs=[slab, slab], out_spec...]
    unnamed x4 -> x0, local copies, waits for them, and re-layouts: 4.6 us -> none
where the time goes in v5:
time: 111 us
  Pallas kernels  111 us (100%)
    pallas_call x1, Pallas kernels, on_device(): pl.pallas_call(functools.partial(kernel, spans, depth, scale), in_specs=[...  106 us
    pallas_call x1, Pallas kernels, on_device(): pl.pallas_call(deliver_kernel, grid=(4,), in_specs=[slab, slab], out_spec...  4.68 us

profile of v5, /device:TPU:0, one launch (start us, length us, event | category | flops | bytes accessed | tf_op | source)
XLA Modules:
  0.0 111.3 jit_solution(4420278759214596321)
XLA Ops:
  0.6 105.9 %grads.1 = (bf16[256,4096]{1,0:T(8,128)(2,1)}, bf16[256,4096]{1,0:T(8,128)(2,1)}) custom-call(bf16[256,4096]{1,0:T(8,128)(2,1)} %q_hbm.1, bf16[256,4096]{1,0:T(8,128)(2,1)} %k_hbm.1, bf16[256,2048]{1,0:T(8,128)(2,1)} %v_hbm.1, bf16[2048,256]{1,0:T(8,128)(2,1)} %teacher_ref.1), custom_call_target="tpu_custom_call" | custom-call | tf_op jit(solution)/shard_map/grads/pallas_call | solution.py:445
  106.6 4.7 %deliver.1 = (bf16[256,4096]{1,0:T(8,128)(2,1)}, bf16[256,4096]{1,0:T(8,128)(2,1)}) custom-call(bf16[256,4096]{1,0:T(8,128)(2,1)} %get-tuple-element.4.q_in, bf16[256,4096]{1,0:T(8,128)(2,1)} %get-tuple-element.5.k_in), custom_call_target="tpu_custom_call" | custom-call | tf_op jit(solution)/shard_map/deliver/pallas_call | solution.py:457

commit v6 on v5

--- a/solution.py
+++ b/solution.py
@@ -26,6 +26,15 @@
 def split(x):
     hi = x.astype(BF16)
     return hi, (x - hi.astype(F32)).astype(BF16)
+
+
+def beside(a, b):
+    return jnp.concatenate([a, b], axis=1)
+
+
+def fold(x):
+    half = x.shape[1] // 2
+    return x[:, :half] + x[:, half:]
 
 
 def encode(x):
@@ -260,7 +269,7 @@
     for load in loads:
         load.start()
     first, second = scratch[:22], scratch[22:44]
-    (target, numer_ref, denom_ref, hi_ref, lo_ref, dd_ref, kl_ref, t_send, t_recv, t_own) = scratch[44:]
+    (target, numer_ref, denom_ref, dn_ref, dd_ref, kl_ref, t_send, t_recv, t_own) = scratch[44:]
     prefix = Exchange(False, spans, depth, first[6:], first[:6])
     suffix = Exchange(True, spans, depth, second[6:], second[:6])
     ctx, grp, plane, groups = prefix.ctx, prefix.grp, 2 * spans, 2 * depth
@@ -321,29 +330,29 @@
         q_wide = q.astype(F32)
         kv, key_row = read_state(prefix.got, head * per_head, per_head)
         kv_hi, kv_lo = split(kv)
-        numer = numer_ref[head] + dot(q, kv_hi, NN) + dot(q, kv_lo, NN)
+        numer = numer_ref[head] + fold(dot(q, beside(kv_hi, kv_lo), NN))
         denom = denom_ref[head] + jnp.sum(q_wide * key_row, axis=1, keepdims=True)
         inv = 1.0 / denom
         student = numer * inv
         resid = student - target[lax.div(head, per_group), :, cols(lax.rem(head, per_group), width)].astype(F32)
         d_denom = -jnp.sum(resid * student, axis=1, keepdims=True) * inv
         dn_hi, dn_lo = split(resid * inv)
-        hi_ref[head] = dn_hi
-        lo_ref[head] = dn_lo
+        dn = beside(dn_hi, dn_lo)
+        dn_ref[head] = dn
         dd_ref[head] = d_denom
-        adj = dot(q, dn_hi, TN) + dot(q, dn_lo, TN)
+        adj = fold(dot(q, dn, TN))
         write_state(suffix.sent, head * per_head, adj, jnp.sum(d_denom * q_wide, axis=0, keepdims=True))
         suffix.send(chunk, d)
 
     def grads_of(head):
         q, k, v = q_ref[:, cols(head, feat)], k_ref[:, cols(head, feat)], v_ref[:, cols(head, width)]
-        dn_hi, dn_lo, d_denom = hi_ref[head], lo_ref[head], dd_ref[head]
+        dn, d_denom = dn_ref[head], dd_ref[head]
         kv, key_row = read_state(prefix.got, head * per_head, per_head)
         kv_hi, kv_lo = split(kv)
-        mixed = jnp.where(causal, dot(dn_hi, v, NT) + dot(dn_lo, v, NT) + d_denom, 0.0)
+        mixed = jnp.where(causal, dot(dn, beside(v, v), NT) + d_denom, 0.0)
         m_hi, m_lo = split(mixed)
         q_grad = dot(m_hi, k, NN) + dot(m_lo, k, NN)
-        q_grad = q_grad + dot(dn_hi, kv_hi, NT) + dot(dn_hi, kv_lo, NT) + dot(dn_lo, kv_hi, NT)
+        q_grad = q_grad + dot(dn, beside(kv_hi, kv_hi), NT) + dot(dn[:, :width], kv_lo, NT)
         q_grad = q_grad + d_denom * key_row
         qg_ref[:, cols(head, feat)] = (scale * q_grad).astype(BF16)
         kl_ref[head] = dot(m_hi, q, TN) + dot(m_lo, q, TN)
@@ -352,7 +361,7 @@
         grads_of(lax.rem(i, plane) * heads_each + lax.div(i, plane))
 
     steps, begin = prefix.steps, depth + 2
-    quick, slow = 4, min(2, H // steps)
+    quick, slow = 4, -(-H // (steps - 1))
 
     def scores_at(t):
         @pl.when(t < H // quick)
@@ -383,22 +392,24 @@
         @pl.when(t >= begin)
         def _():
             for i in range(slow):
-                grads_at(slow * (t - begin) + i)
+                at = slow * (t - begin) + i
+
+                @pl.when(at < H)
+                def _(at=at):
+                    grads_at(at)
 
         return unused
 
     loads[2].wait()
     scores_at(0)
     lax.fori_loop(0, begin + steps, step, 0)
-    for i in range(slow * steps, H):
-        grads_of(i % plane * heads_each + i // plane)
 
     def backward(head, chunk, d):
         suffix.receive(chunk, d)
         adj, row = read_state(suffix.got, head * per_head, per_head)
         a_hi, a_lo = split(adj)
         v = v_ref[:, cols(head, width)]
-        k_grad = kl_ref[head] + dot(v, a_hi, NT) + dot(v, a_lo, NT) + row
+        k_grad = kl_ref[head] + dot(beside(v, v), beside(a_hi, a_lo), NT) + row
         kg_ref[:, cols(head, feat)] = (scale * k_grad).astype(BF16)
 
     for group in range(heads_each):
@@ -432,12 +443,12 @@
     phase = [wide] * 3 + [row] * 3 + [whole] * 2 + [pairs, block] + [line] * 4
     phase += [dma((chunks // 2, plane - 1))] * 2 + [dma((chunks, plane - 1))] * 2 + [dma((chunks,))] * 4
     column = pltpu.VMEM((H, rows, 1), F32)
-    half = pltpu.VMEM((H, rows, width), BF16)
+    both = pltpu.VMEM((H, rows, 2 * width), BF16)
     scratch = [pltpu.VMEM(x.shape, BF16) for x in (query_feat, key_feat, values)] + [dma((3,))]
     scratch += phase + phase + [
         pltpu.VMEM((groups, rows, teacher.shape[1]), BF16),
         pltpu.VMEM((H, rows, width), F32),
-        column, half, half, column,
+        column, both, column,
         pltpu.VMEM((H, rows, feat), F32),
         dma((groups - 1,)), dma((groups - 1,)), dma,
     ]

time: 111 us -> 110 us (level)
  Pallas kernels: 111 us -> 109 us
    pallas_call x1, Pallas kernels: 106 us -> 104 us  [on_device(): pl.pallas_call(functools.partial(kernel, spans, depth, scale), in_specs=[...]
where the time goes in v6:
time: 110 us
  Pallas kernels  109 us (99%)
    pallas_call x1, Pallas kernels, on_device(): pl.pallas_call(functools.partial(kernel, spans, depth, scale), in_specs=[...  104 us
    pallas_call x1, Pallas kernels, on_device(): pl.pallas_call(deliver_kernel, grid=(4,), in_specs=[slab, slab], out_spec...  4.68 us

profile of v6, /device:TPU:0, one launch (start us, length us, event | category | flops | bytes accessed | tf_op | source)
XLA Modules:
  0.0 109.7 jit_solution(4040996465415946710)
XLA Ops:
  0.6 104.4 %grads.1 = (bf16[256,4096]{1,0:T(8,128)(2,1)}, bf16[256,4096]{1,0:T(8,128)(2,1)}) custom-call(bf16[256,4096]{1,0:T(8,128)(2,1)} %q_hbm.1, bf16[256,4096]{1,0:T(8,128)(2,1)} %k_hbm.1, bf16[256,2048]{1,0:T(8,128)(2,1)} %v_hbm.1, bf16[2048,256]{1,0:T(8,128)(2,1)} %teacher_ref.1), custom_call_target="tpu_custom_call" | custom-call | tf_op jit(solution)/shard_map/grads/pallas_call | solution.py:456
  105.0 4.7 %deliver.1 = (bf16[256,4096]{1,0:T(8,128)(2,1)}, bf16[256,4096]{1,0:T(8,128)(2,1)}) custom-call(bf16[256,4096]{1,0:T(8,128)(2,1)} %get-tuple-element.4.q_in, bf16[256,4096]{1,0:T(8,128)(2,1)} %get-tuple-element.5.k_in), custom_call_target="tpu_custom_call" | custom-call | tf_op jit(solution)/shard_map/deliver/pallas_call | solution.py:468
